TPU v7x, 256 devices: a whole 4x4x8 slice. The times are simulated.
256 devices in a mesh: row: 16 (over z_hi, x), col: 16 (over z_lo, y, core).
Axes of the slice: x: 4, y: 4, z: 8 (z_hi: 4, z_lo: 2; z = z_hi * 2 + z_lo), core: 2. Of those that a mesh axis runs over, the one named last changes fastest.
Arguments:
- values: bfloat16 [16, 16, 2, 18, 128, 128], P('row', 'col'), may hold values from -6 to 6
- mask_x: int32 [16, 16, 2, 18], P('row', 'col'), may hold values from 0 to 1, as said below
- mask_sq: int32 [16, 16, 2, 26], P('row', 'col'), may hold values from 0 to 1, as said below
Outputs:
- result: bfloat16 [16, 16, 2, 18, 128, 128], P('row', 'col')
Inputs may be any that keep to these rules, and one draw needn't show every extreme that they name: `mask_x`: in every row the slot of offset (0, 0) and the row's own layer is 1, and at least one row has all 18 slots equal to 1. `mask_sq`: 1 wherever mask_x is 1 in the slot with the same offset and layer.
All inputs are finite; a program needn't handle non-finite values.
Results may differ from a plain program's by a relative error of at most 0.0033.
Values may be sent and summed in bfloat16 or wider, within the bound.
A program may use at most 64 MiB of HBM per device.

v0:
```python
import jax
import jax.numpy as jnp
from jax import lax
from jax.sharding import PartitionSpec as P

given_offsets = [(u, v) for u in (-1, 0, 1) for v in (-1, 0, 1)]
square_offsets = [(u, v) for u in range(-2, 3) for v in range(-2, 3) if u * u + v * v <= 4]


def padded_2(cells, sides, width):
    for axis, dim in sides:
        count = lax.axis_size(axis)
        head = lax.slice_in_dim(cells, 0, width, axis=dim)
        tail = lax.slice_in_dim(cells, cells.shape[dim] - width, cells.shape[dim], axis=dim)
        cells = jnp.concatenate(
            [
                lax.ppermute(tail, axis, [(i, (i + 1) % count) for i in range(count)]),
                cells,
                lax.ppermute(head, axis, [((i + 1) % count, i) for i in range(count)]),
            ],
            axis=dim,
        )
    return cells


def combine(left_blocks, neighbour_rows, out_offsets, left_offsets, right_offsets, layers, finish):
    outputs = []
    for target_index, target in enumerate(out_offsets):
        total = None
        for position, (p, q) in enumerate(left_offsets):
            remainder = (target[0] - p, target[1] - q)
            if remainder in right_offsets:
                left_part = left_blocks[:, :, :, position * layers : (position + 1) * layers]
                right_part = neighbour_rows(p, q, right_offsets.index(remainder) * layers, layers)
                term = jnp.einsum(
                    "abikxy,abkmyz->abimxz",
                    left_part,
                    right_part,
                    preferred_element_type=jnp.float32,
                )
                total = term if total is None else total + term
        outputs.append(finish(target_index, total))
    return jnp.concatenate(outputs, axis=3)


def local(values, mask_x, mask_sq):
    layers = values.shape[2]
    columns_here = values.shape[1]
    masked = jnp.where(mask_x[..., None, None] > 0, values, jnp.zeros_like(values))
    padded = padded_2(masked, (("row", 0), ("col", 1)), 1)

    def given_rows(s, t, start, count):
        return padded[1 + s : 2 + s, 1 + t : 1 + t + columns_here, :, start : start + count]

    weight = 0.25 / values.shape[-1]

    def finish_square(target_index, total):
        keep = mask_sq[:, :, :, target_index * layers : (target_index + 1) * layers]
        return jnp.where(keep[..., None, None] > 0, total * weight, jnp.float32(0.0)).astype(
            jnp.bfloat16
        )

    filtered = combine(
        masked, given_rows, square_offsets, given_offsets, given_offsets, layers, finish_square
    )
    square_pad = padded_2(filtered, (("row", 0), ("col", 1)), 1)

    def square_rows(s, t, start, count):
        return square_pad[1 + s : 2 + s, 1 + t : 1 + t + columns_here, :, start : start + count]

    def finish_cube(target_index, total):
        own = masked[:, :, :, target_index * layers : (target_index + 1) * layers]
        keep = mask_x[:, :, :, target_index * layers : (target_index + 1) * layers]
        return jnp.where(
            keep[..., None, None] > 0, 1.5 * own.astype(jnp.float32) - 0.5 * total, jnp.float32(0.0)
        ).astype(jnp.bfloat16)

    return combine(
        masked, square_rows, given_offsets, given_offsets, square_offsets, layers, finish_cube
    )


def solution(mesh):
    return jax.shard_map(
        local,
        mesh=mesh,
        in_specs=(
            P("row", "col", None, None, None, None),
            P("row", "col", None, None),
            P("row", "col", None, None),
        ),
        out_specs=P("row", "col", None, None, None, None),
        check_vma=False,
    )
```

profile of v0, /device:TPU:32, one launch (start us, length us, event | category | flops | bytes accessed | tf_op | source)
XLA Modules:
  0.0 261.8 jit_solution(3799921699575687611)
XLA Ops:
  0.0 0.7 compare_bitcast_fusion.21
  0.7 1.4 broadcast_select_fusion
  2.1 1.6 collective-permute-start
  3.7 6.2 %collective-permute-start.1 = (bf16[1,1,2,18,128,128]{5,4,3,2,1,0:T(8,128)(2,1)S(1)}, bf16[1,1,2,18,128,128]{5,4,3,2,1,0:T(8,128)(2,1)S(1)}, u32[]{:S(2)}, u32[]{:S(2)}) collective-permute-start(bf16[1,1,2,18,128,128]{5,4,3,2,1,0:T(8,128)(2,1)S(1)} %broadcast_select_fusion), channel_id=1, source_target_pairs={{16,0},{32,16},{48,32},{64,48},{80,64},{96,80},{112,96},{128,112},... | collective-permute-start | bytes 3538952 | tf_op jit(solution)/shard_map/ppermute | solution.py:19
  9.9 51.2 %collective-permute-done = bf16[1,1,2,18,128,128]{5,4,3,2,1,0:T(8,128)(2,1)S(1)} collective-permute-done((bf16[1,1,2,18,128,128]{5,4,3,2,1,0:T(8,128)(2,1)S(1)}, bf16[1,1,2,18,128,128]{5,4,3,2,1,0:T(8,128)(2,1)S(1)}, u32[]{:S(2)}, u32[]{:S(2)}) %collective-permute-start) | collective-permute-done | bytes 1179680 | tf_op jit(solution)/shard_map/ppermute | solution.py:17
  61.0 0.4 pad_maximum_fusion.1
  61.5 1.8 collective-permute-start.3
  65.1 0.2 convolution_bitcast_fusion.120
  65.3 0.2 convolution_bitcast_fusion.117
  65.5 0.2 convolution_bitcast_fusion.113
  66.1 0.2 convolution_bitcast_fusion.88
  66.3 0.2 convolution_bitcast_fusion.94
  66.5 0.2 convolution_bitcast_fusion.82
  66.7 0.2 convolution_bitcast_fusion.74
  66.9 0.2 convolution_bitcast_fusion.69
  67.1 0.2 convolution_bitcast_fusion.65
  67.3 0.2 convolution_bitcast_fusion.62
  67.4 34.8 %collective-permute-done.3 = bf16[3,1,2,18,128,128]{5,4,3,2,1,0:T(8,128)(2,1)S(1)} collective-permute-done((bf16[3,1,2,18,128,128]{5,4,3,2,1,0:T(8,128)(2,1)S(1)}, bf16[3,1,2,18,128,128]{5,4,3,2,1,0:T(8,128)(2,1)S(1)}, u32[]{:S(2)}, u32[]{:S(2)}) %collective-permute-start.3) | collective-permute-done | bytes 3538976 | tf_op jit(solution)/shard_map/ppermute | solution.py:19
  102.7 3.6 %collective-permute-done.2 = bf16[3,1,2,18,128,128]{5,4,3,2,1,0:T(8,128)(2,1)S(1)} collective-permute-done((bf16[3,1,2,18,128,128]{5,4,3,2,1,0:T(8,128)(2,1)S(1)}, bf16[3,1,2,18,128,128]{5,4,3,2,1,0:T(8,128)(2,1)S(1)}, u32[]{:S(2)}, u32[]{:S(2)}) %collective-permute-start.2) | collective-permute-done | bytes 3538976 | tf_op jit(solution)/shard_map/ppermute | solution.py:17
  111.1 0.2 fusion.209
  111.3 0.3 constant_dynamic-update-slice_fusion.8
  111.6 0.3 constant_dynamic-update-slice_fusion.7
  111.9 0.3 constant_dynamic-update-slice_fusion.6
  112.1 0.2 fusion.202
  112.4 0.3 constant_dynamic-update-slice_fusion.5
  112.6 0.3 constant_dynamic-update-slice_fusion.4
  113.0 0.3 constant_dynamic-update-slice_fusion.3
  113.3 0.2 fusion.199
  113.5 0.2 constant_dynamic-update-slice_fusion.2
  113.8 0.3 constant_dynamic-update-slice_fusion.1
  114.1 0.3 constant_dynamic-update-slice_fusion
  114.3 0.2 fusion.192
  114.6 7.0 %collective-permute-start.5 = (bf16[1,1,2,26,128,128]{5,4,3,2,1,0:T(8,128)(2,1)S(1)}, bf16[1,1,2,26,128,128]{5,4,3,2,1,0:T(8,128)(2,1)S(1)}, u32[]{:S(2)}, u32[]{:S(2)}) collective-permute-start(bf16[1,1,2,26,128,128]{5,4,3,2,1,0:T(8,128)(2,1)S(1)} %fusion.192), channel_id=1, source_target_pairs={{16,0},{32,16},{48,32},{64,48},{80,64},{96,80},{112,96},{128,112},... | collective-permute-start | bytes 5111816 | tf_op jit(solution)/shard_map/ppermute | solution.py:19
  121.6 68.9 %collective-permute-done.4 = bf16[1,1,2,26,128,128]{5,4,3,2,1,0:T(8,128)(2,1)S(1)} collective-permute-done((bf16[1,1,2,26,128,128]{5,4,3,2,1,0:T(8,128)(2,1)S(1)}, bf16[1,1,2,26,128,128]{5,4,3,2,1,0:T(8,128)(2,1)S(1)}, u32[]{:S(2)}, u32[]{:S(2)}) %collective-permute-start.4) | collective-permute-done | bytes 1703968 | tf_op jit(solution)/shard_map/ppermute | solution.py:17
  190.6 0.6 pad_maximum_fusion
  191.2 4.5 %collective-permute-start.7 = (bf16[3,1,2,26,128,128]{5,4,3,2,1,0:T(8,128)(2,1)S(1)}, bf16[3,1,2,26,128,128]{5,4,3,2,1,0:T(8,128)(2,1)S(1)}, u32[]{:S(2)}, u32[]{:S(2)}) collective-permute-start(bf16[3,1,2,26,128,128]{5,4,3,2,1,0:T(8,128)(2,1)S(1)} %pad_maximum_fusion), channel_id=1, source_target_pairs={{1,0},{2,1},{3,2},{4,3},{5,4},{6,5},{7,6},{8,7},{9,8},{10,9},{11,1... | collective-permute-start | bytes 15335432 | tf_op jit(solution)/shard_map/ppermute | solution.py:19
  195.9 0.2 convolution_bitcast_fusion.56
  199.9 51.6 %collective-permute-done.6 = bf16[3,1,2,26,128,128]{5,4,3,2,1,0:T(8,128)(2,1)S(1)} collective-permute-done((bf16[3,1,2,26,128,128]{5,4,3,2,1,0:T(8,128)(2,1)S(1)}, bf16[3,1,2,26,128,128]{5,4,3,2,1,0:T(8,128)(2,1)S(1)}, u32[]{:S(2)}, u32[]{:S(2)}) %collective-permute-start.6) | collective-permute-done | bytes 5111840 | tf_op jit(solution)/shard_map/ppermute | solution.py:17
  257.5 0.3 fusion.179
  257.8 0.3 fusion.177
  258.1 0.3 fusion.175
  258.4 0.3 fusion.173
  258.7 0.3 fusion.171
  259.0 0.3 fusion.169
  259.3 0.3 fusion.167
  259.6 0.3 fusion.165
  259.9 1.0 copy-done.2
  260.9 0.9 fusion.163
  (102 shorter events, 16.7 us)
Async XLA Ops:
  2.1 58.9 %collective-permute-start = (bf16[1,1,2,18,128,128]{5,4,3,2,1,0:T(8,128)(2,1)S(1)}, bf16[1,1,2,18,128,128]{5,4,3,2,1,0:T(8,128)(2,1)S(1)}, u32[]{:S(2)}, u32[]{:S(2)}) collective-permute-start(bf16[1,1,2,18,128,128]{5,4,3,2,1,0:T(8,128)(2,1)S(1)} %broadcast_select_fusion), channel_id=1, source_target_pairs={{0,16},{16,32},{32,48},{48,64},{64,80},{80,96},{96,112},{112,128},... | collective-permute-start | bytes 3538952 | tf_op jit(solution)/shard_map/ppermute | solution.py:17
  3.7 57.4 %collective-permute-start.1 = (bf16[1,1,2,18,128,128]{5,4,3,2,1,0:T(8,128)(2,1)S(1)}, bf16[1,1,2,18,128,128]{5,4,3,2,1,0:T(8,128)(2,1)S(1)}, u32[]{:S(2)}, u32[]{:S(2)}) collective-permute-start(bf16[1,1,2,18,128,128]{5,4,3,2,1,0:T(8,128)(2,1)S(1)} %broadcast_select_fusion), channel_id=1, source_target_pairs={{16,0},{32,16},{48,32},{64,48},{80,64},{96,80},{112,96},{128,112},... | collective-permute-start | bytes 3538952 | tf_op jit(solution)/shard_map/ppermute | solution.py:19
  61.5 40.8 %collective-permute-start.3 = (bf16[3,1,2,18,128,128]{5,4,3,2,1,0:T(8,128)(2,1)S(1)}, bf16[3,1,2,18,128,128]{5,4,3,2,1,0:T(8,128)(2,1)S(1)}, u32[]{:S(2)}, u32[]{:S(2)}) collective-permute-start(bf16[3,1,2,18,128,128]{5,4,3,2,1,0:T(8,128)(2,1)S(1)} %pad_maximum_fusion.1), channel_id=1, source_target_pairs={{1,0},{2,1},{3,2},{4,3},{5,4},{6,5},{7,6},{8,7},{9,8},{10,9},{11,1... | collective-permute-start | bytes 10616840 | tf_op jit(solution)/shard_map/ppermute | solution.py:19
  63.3 43.0 %collective-permute-start.2 = (bf16[3,1,2,18,128,128]{5,4,3,2,1,0:T(8,128)(2,1)S(1)}, bf16[3,1,2,18,128,128]{5,4,3,2,1,0:T(8,128)(2,1)S(1)}, u32[]{:S(2)}, u32[]{:S(2)}) collective-permute-start(bf16[3,1,2,18,128,128]{5,4,3,2,1,0:T(8,128)(2,1)S(1)} %pad_maximum_fusion.1), channel_id=1, source_target_pairs={{0,1},{1,2},{2,3},{3,4},{4,5},{5,6},{6,7},{7,8},{8,9},{9,10},{10,1... | collective-permute-start | bytes 10616840 | tf_op jit(solution)/shard_map/ppermute | solution.py:17
  64.1 1.0 copy-start
  114.5 81.2 %copy-start.1 = (s32[1,1,2,18]{3,2,1,0:T(2,128)S(1)}, s32[1,1,2,18]{3,2,1,0:T(2,128)}, u32[]{:S(2)}) copy-start(s32[1,1,2,18]{3,2,1,0:T(2,128)} %param.4) | copy-start | bytes 436
  114.6 76.0 %collective-permute-start.4 = (bf16[1,1,2,26,128,128]{5,4,3,2,1,0:T(8,128)(2,1)S(1)}, bf16[1,1,2,26,128,128]{5,4,3,2,1,0:T(8,128)(2,1)S(1)}, u32[]{:S(2)}, u32[]{:S(2)}) collective-permute-start(bf16[1,1,2,26,128,128]{5,4,3,2,1,0:T(8,128)(2,1)S(1)} %fusion.192), channel_id=1, source_target_pairs={{0,16},{16,32},{32,48},{48,64},{64,80},{80,96},{96,112},{112,128},... | collective-permute-start | bytes 5111816 | tf_op jit(solution)/shard_map/ppermute | solution.py:17
  114.6 75.9 %collective-permute-start.5 = (bf16[1,1,2,26,128,128]{5,4,3,2,1,0:T(8,128)(2,1)S(1)}, bf16[1,1,2,26,128,128]{5,4,3,2,1,0:T(8,128)(2,1)S(1)}, u32[]{:S(2)}, u32[]{:S(2)}) collective-permute-start(bf16[1,1,2,26,128,128]{5,4,3,2,1,0:T(8,128)(2,1)S(1)} %fusion.192), channel_id=1, source_target_pairs={{16,0},{32,16},{48,32},{64,48},{80,64},{96,80},{112,96},{128,112},... | collective-permute-start | bytes 5111816 | tf_op jit(solution)/shard_map/ppermute | solution.py:19
  191.2 60.4 %collective-permute-start.6 = (bf16[3,1,2,26,128,128]{5,4,3,2,1,0:T(8,128)(2,1)S(1)}, bf16[3,1,2,26,128,128]{5,4,3,2,1,0:T(8,128)(2,1)S(1)}, u32[]{:S(2)}, u32[]{:S(2)}) collective-permute-start(bf16[3,1,2,26,128,128]{5,4,3,2,1,0:T(8,128)(2,1)S(1)} %pad_maximum_fusion), channel_id=1, source_target_pairs={{0,1},{1,2},{2,3},{3,4},{4,5},{5,6},{6,7},{7,8},{8,9},{9,10},{10,1... | collective-permute-start | bytes 15335432 | tf_op jit(solution)/shard_map/ppermute | solution.py:17
  191.2 60.7 %collective-permute-start.7 = (bf16[3,1,2,26,128,128]{5,4,3,2,1,0:T(8,128)(2,1)S(1)}, bf16[3,1,2,26,128,128]{5,4,3,2,1,0:T(8,128)(2,1)S(1)}, u32[]{:S(2)}, u32[]{:S(2)}) collective-permute-start(bf16[3,1,2,26,128,128]{5,4,3,2,1,0:T(8,128)(2,1)S(1)} %pad_maximum_fusion), channel_id=1, source_target_pairs={{1,0},{2,1},{3,2},{4,3},{5,4},{6,5},{7,6},{8,7},{9,8},{10,9},{11,1... | collective-permute-start | bytes 15335432 | tf_op jit(solution)/shard_map/ppermute | solution.py:19
  259.9 1.0 copy-start.2
where the time goes:
time: 265 us; the launch traced here: 262 us
  waiting for transfers between devices  210 us (79%)
  matrix products  25.1 us (9%)
  starting transfers between devices  21.3 us (8%)
  other arithmetic  3.25 us (1%)
    ppermute x4, waiting for transfers between devices, padded_2(): lax.ppermute(tail, axis, [(i, (i + 1) % count) for i in range(count)])  175 us
    ppermute x4, waiting for transfers between devices, padded_2(): lax.ppermute(head, axis, [((i + 1) % count, i) for i in range(count)])  34.8 us
    dot_general x122, matrix products, combine(): jnp.einsum('abikxy,abkmyz->abimxz', left_part, right_part, preferred_elem...  25.1 us
    ppermute x4, starting transfers between devices, padded_2(): lax.ppermute(head, axis, [((i + 1) % count, i) for i in range(count)])  19.5 us
  transfers between devices with their start and end apart: 8, of which 5 were waited for; matrix products, arithmetic and copies ran while one was open for 3% of the time, Pallas kernels for 0%

commit v1 on v0

v1 whole, which is shorter than its diff:
```python
import jax
import jax.numpy as jnp
from jax import lax
from jax.experimental import pallas as pl
from jax.experimental.pallas import tpu as pltpu
from jax.sharding import PartitionSpec as P

BS = 128
UNIT = 2 * BS
MESH = pl.DeviceIdType.MESH

square_units = [(0, -2), (0, 2)] + [(u, 0) for u in range(-2, 3)]
square_units += [(u, -1) for u in (-1, 0, 1)] + [(u, 1) for u in (-1, 0, 1)]
square_at = {t: n for n, t in enumerate(square_units)}
square_slots = [(u, v) for u in range(-2, 3) for v in range(-2, 3) if u * u + v * v <= 4]

left_square = [(u, 0) for u in range(-2, 3)] + [(0, 2)] + [(u, 1) for u in (-1, 0, 1)]
right_square = [(u, 0) for u in range(-2, 3)] + [(0, -2)] + [(u, -1) for u in (-1, 0, 1)]
left_cube = [(u, v) for v in (-1, 1, 0) for u in (-1, 0, 1)]
right_cube = [(u, v) for v in (1, -1, 0) for u in (-1, 0, 1)]


def given_at(u, v):
    return (v + 1) * 3 + u + 1


def make_kernel(rows, cols):
    def kernel(
        values, mask_x, mask_sq, out,
        staged, own, above, below, from_left, from_right,
        give_left, give_right, got_left, got_right,
        filtered, filt_above, filt_below,
        give_left2, give_right2, got_left2, got_right2,
        acc, result, load_sem, out_sem, send_sem, recv_sem,
    ):
        a, b = lax.axis_index("row"), lax.axis_index("col")
        up = (lax.rem(a + rows - 1, rows), b)
        down = (lax.rem(a + 1, rows), b)
        left = (a, lax.rem(b + cols - 1, cols))
        right = (a, lax.rem(b + 1, cols))

        loads = {}
        for c in (0, 2, 1):
            loads[c] = pltpu.make_async_copy(values.at[:, :, c], staged.at[c], load_sem.at[c])
            loads[c].start()

        barrier = pltpu.get_barrier_semaphore()
        for device in (up, down, left, right):
            pl.semaphore_signal(barrier, inc=1, device_id=device, device_id_type=MESH)
        pl.semaphore_wait(barrier, 4)

        sent = []

        def send(src, dst, device):
            n = len(sent)
            copy = pltpu.make_async_remote_copy(
                src_ref=src, dst_ref=dst, send_sem=send_sem.at[n], recv_sem=recv_sem.at[n],
                device_id=device, device_id_type=MESH,
            )
            copy.start()
            sent.append(copy)
            return copy

        def blocks(ref, unit):
            for l in range(2):
                for m in range(2):
                    yield l, m, ref.at[unit, pl.ds(l * BS, BS), pl.ds(m * BS, BS)]

        vertical = {}
        for c in (0, 2, 1):
            loads[c].wait()
            for ui in range(3):
                for l, m, block in blocks(own, c * 3 + ui):
                    keep = mask_x[0, 0, l, (ui * 3 + c) * 2 + m] > 0
                    value = staged[c, l, ui, m]
                    block[...] = jnp.where(keep, value, jnp.zeros_like(value))
            span = pl.ds(c * 3, 3)
            vertical[c] = (
                send(own.at[span], below.at[span], up),
                send(own.at[span], above.at[span], down),
            )
            if c == 0:
                to_left = send(own.at[span], from_right, left)
            if c == 2:
                to_right = send(own.at[span], from_left, right)

        row_of = {-1: above, 0: own, 1: below}
        filt_of = {
            -1: (filt_above, lambda u, v: down_units.index((u, v))),
            0: (filtered, lambda u, v: square_at[(u, v)]),
            1: (filt_below, lambda u, v: up_units.index((u, v))),
        }
        factor = {
            1: lambda p: from_left[p + 1],
            -1: lambda p: from_right[p + 1],
            0: lambda p: own[given_at(p, 0)],
        }

        def product_square(q, t):
            total = None
            for p in (-1, 0, 1):
                u, v = t[0] - p, t[1] - q
                if abs(u) <= 1 and abs(v) <= 1:
                    term = jnp.dot(
                        factor[q](p), row_of[p][given_at(u, v)], preferred_element_type=jnp.float32
                    )
                    total = term if total is None else total + term
            return total

        def product_cube(q, t):
            total = None
            for p in (-1, 0, 1):
                u, v = t[0] - p, t[1] - q
                if u * u + v * v <= 4:
                    ref, place = filt_of[p]
                    term = jnp.dot(factor[q](p), ref[place(u, v)], preferred_element_type=jnp.float32)
                    total = term if total is None else total + term
            return total

        def give(product, q, order, targets, buffer, landing, device):
            first = order.index(targets[0])
            for n, t in enumerate(targets):
                buffer[first + n] = product(q, t).astype(jnp.bfloat16)
            span = pl.ds(first, len(targets))
            return send(buffer.at[span], landing.at[span], device)

        def give_left_square(targets):
            return give(product_square, 1, left_square, targets, give_left, got_right, left)

        def give_right_square(targets):
            return give(product_square, -1, right_square, targets, give_right, got_left, right)

        def finish_square(t, total):
            s = square_at[t]
            if t in left_square:
                part = got_right[left_square.index(t)].astype(jnp.float32)
                total = part if total is None else total + part
            if t in right_square:
                part = got_left[right_square.index(t)].astype(jnp.float32)
                total = part if total is None else total + part
            total = total * (0.25 / BS)
            for l, m, block in blocks(filtered, s):
                keep = mask_sq[0, 0, l, square_slots.index(t) * 2 + m] > 0
                value = total[l * BS : (l + 1) * BS, m * BS : (m + 1) * BS]
                block[...] = jnp.where(keep, value, jnp.zeros_like(value)).astype(jnp.bfloat16)

        up_units = [(0, -2), (0, 2)] + [(u, 0) for u in (-2, -1, 0)]
        up_units += [(u, v) for v in (-1, 1) for u in (-1, 0)]
        down_units = [(0, -2), (0, 2)] + [(u, 0) for u in (0, 1, 2)]
        down_units += [(u, v) for v in (-1, 1) for u in (0, 1)]

        def send_filtered(units_up, units_down):
            copies = []
            for units, order, landing, device in (
                (units_up, up_units, filt_below, up),
                (units_down, down_units, filt_above, down),
            ):
                copies.append(
                    send(
                        filtered.at[pl.ds(square_at[units[0]], len(units))],
                        landing.at[pl.ds(order.index(units[0]), len(units))],
                        device,
                    )
                )
            return copies

        def await_recv(*copies):
            for copy in copies:
                copy.wait_recv()

        await_recv(to_left, to_right)
        await_recv(*vertical[0])
        r_far = give_right_square([(0, -2)])
        l_mid = give_left_square([(u, 0) for u in range(-2, 3)])
        await_recv(r_far)
        finish_square((0, -2), None)
        f_left = send_filtered([(0, -2)], [(0, -2)])
        await_recv(*vertical[2])
        l_far = give_left_square([(0, 2)])
        r_mid = give_right_square([(u, 0) for u in range(-2, 3)])
        await_recv(l_far)
        finish_square((0, 2), None)
        f_right = send_filtered([(0, 2)], [(0, 2)])
        for n, v in enumerate((-1, 1)):
            for u in (-1, 0, 1):
                acc[n * 3 + u + 1] = product_square(0, (u, v))
        await_recv(*vertical[1])
        near = []
        for u in (0, -1, 1):
            near.append(give_left_square([(u, 1)]))
            near.append(give_right_square([(u, -1)]))
        await_recv(l_mid, r_mid)
        for u in range(-2, 3):
            finish_square((u, 0), product_square(0, (u, 0)))
        f_mid = send_filtered([(u, 0) for u in (-2, -1, 0)], [(u, 0) for u in (0, 1, 2)])
        await_recv(*near)
        f_near = []
        for n, v in enumerate((-1, 1)):
            for u in (-1, 0, 1):
                finish_square((u, v), acc[n * 3 + u + 1])
            f_near.append(send_filtered([(u, v) for u in (-1, 0)], [(u, v) for u in (0, 1)]))

        def give_left_cube(v):
            return give(
                product_cube, 1, left_cube, [(u, v) for u in (-1, 0, 1)], give_left2, got_right2, left
            )

        def give_right_cube(v):
            return give(
                product_cube, -1, right_cube, [(u, v) for u in (-1, 0, 1)], give_right2, got_left2, right
            )

        def finish_cube(t, total):
            u, v = t
            total = total + got_right2[left_cube.index(t)].astype(jnp.float32)
            total = total + got_left2[right_cube.index(t)].astype(jnp.float32)
            total = 1.5 * own[given_at(u, v)].astype(jnp.float32) - 0.5 * total
            for l in range(2):
                for m in range(2):
                    keep = mask_x[0, 0, l, ((u + 1) * 3 + v + 1) * 2 + m] > 0
                    value = total[l * BS : (l + 1) * BS, m * BS : (m + 1) * BS]
                    result[v + 1, l, u + 1, m] = jnp.where(keep, value, jnp.zeros_like(value)).astype(
                        jnp.bfloat16
                    )

        stores = []

        def store(v):
            copy = pltpu.make_async_copy(result.at[v + 1], out.at[:, :, v + 1], out_sem.at[v + 1])
            copy.start()
            stores.append(copy)

        await_recv(*f_left)
        c_l = [give_left_cube(-1)]
        await_recv(*f_right)
        c_r = [give_right_cube(1)]
        await_recv(*f_mid)
        c_l.append(give_left_cube(1))
        c_r.append(give_right_cube(-1))
        for u in (-1, 0, 1):
            acc[6 + u + 1] = product_cube(0, (u, 0))
        await_recv(*f_near[0])
        c_l.append(give_left_cube(0))
        await_recv(*f_near[1])
        c_r.append(give_right_cube(0))
        await_recv(c_l[0], c_l[1], c_r[0], c_r[1])
        for v in (-1, 1):
            for u in (-1, 0, 1):
                finish_cube((u, v), product_cube(0, (u, v)))
            store(v)
        await_recv(c_l[2], c_r[2])
        for u in (-1, 0, 1):
            finish_cube((u, 0), acc[6 + u + 1])
        store(0)
        for copy in sent:
            copy.wait_send()
        for copy in stores:
            copy.wait()

    return kernel


def solution(mesh):
    rows, cols = mesh.shape["row"], mesh.shape["col"]

    def units(n, dtype=jnp.bfloat16):
        return pltpu.VMEM((n, UNIT, UNIT), dtype)

    def local(values, mask_x, mask_sq):
        grid = values.reshape(2, 3, 3, 2, BS, BS)
        out = pl.pallas_call(
            make_kernel(rows, cols),
            out_shape=jax.ShapeDtypeStruct(grid.shape, jnp.bfloat16),
            in_specs=[
                pl.BlockSpec(memory_space=pl.ANY),
                pl.BlockSpec(memory_space=pltpu.SMEM),
                pl.BlockSpec(memory_space=pltpu.SMEM),
            ],
            out_specs=pl.BlockSpec(memory_space=pl.ANY),
            scratch_shapes=[
                pltpu.VMEM((3, 2, 3, 2, BS, BS), jnp.bfloat16),
                units(9), units(9), units(9), units(3), units(3),
                units(9), units(9), units(9), units(9),
                units(13), units(9), units(9),
                units(9), units(9), units(9), units(9),
                units(9, jnp.float32),
                pltpu.VMEM((3, 2, 3, 2, BS, BS), jnp.bfloat16),
                pltpu.SemaphoreType.DMA((3,)),
                pltpu.SemaphoreType.DMA((3,)),
                pltpu.SemaphoreType.DMA((40,)),
                pltpu.SemaphoreType.DMA((40,)),
            ],
            compiler_params=pltpu.CompilerParams(
                collective_id=0, has_side_effects=True, vmem_limit_bytes=48 * 2**20
            ),
        )(grid, mask_x, mask_sq)
        return out.reshape(values.shape)

    return jax.shard_map(
        local,
        mesh=mesh,
        in_specs=(
            P("row", "col", None, None, None, None),
            P("row", "col", None, None),
            P("row", "col", None, None),
        ),
        out_specs=P("row", "col", None, None, None, None),
        check_vma=False,
    )
```

time: 265 us -> 148 us (0.56)
  the two profiles are of different devices: /device:TPU:32 before, /device:TPU:166 now
where the time goes in v1:
time: 148 us; the launch traced here: 147 us
  Pallas kernels  144 us (97%)
  local copies, waits for them, and re-layouts  3.64 us (2%)
    pallas_call x1, Pallas kernels, local(): pl.pallas_call(make_kernel(rows, cols), out_shape=jax.ShapeDtypeStruct(gr...  144 us
    unnamed x7, local copies, waits for them, and re-layouts  3.64 us

profile of v1, /device:TPU:166, one launch (start us, length us, event | category | flops | bytes accessed | tf_op | source)
XLA Modules:
  0.0 147.4 jit_solution(15559302784741656271)
XLA Ops:
  0.0 0.0 copy-start
  0.0 1.3 copy-done
  1.3 0.0 copy-start.1
  1.3 0.7 copy-done.1
  2.0 0.0 copy-start.2
  2.0 0.7 copy-done.2
  2.6 143.8 %shard_map.37 = bf16[2,3,3,2,128,128]{5,4,3,2,1,0:T(8,128)(2,1)S(1)} custom-call(bf16[2,3,3,2,128,128]{5,4,3,2,1,0:T(8,128)(2,1)S(1)} %bitcast.3, s32[1,1,2,18]{3,2,1,0:T(2,128)S(1)} %copy-done.1, s32[1,1,2,26]{3,2,1,0:T(2,128)S(1)} %copy-done.2), custom_call_target="tpu_custom_call" | custom-call | tf_op jit(solution)/shard_map/pallas_call | solution.py:271
  146.4 1.0 copy.5
Async XLA Ops:
  0.0 1.3 copy-start
  1.3 0.7 copy-start.1
  2.0 0.7 copy-start.2

commit v2 on v1

v2 whole, which is shorter than its diff:
```python
import jax
import jax.numpy as jnp
from jax import lax
from jax.experimental import pallas as pl
from jax.experimental.pallas import tpu as pltpu
from jax.sharding import PartitionSpec as P

BS = 128
UNIT = 2 * BS
MESH = pl.DeviceIdType.MESH
X = 4

square_units = [(0, -2), (0, 2)] + [(u, 0) for u in range(-2, 3)]
square_units += [(u, -1) for u in (-1, 0, 1)] + [(u, 1) for u in (-1, 0, 1)]
up_units = [(0, -2), (0, 2)] + [(u, 0) for u in (-2, -1, 0)]
up_units += [(u, v) for v in (-1, 1) for u in (-1, 0)]
down_units = [(0, -2), (0, 2)] + [(u, 0) for u in (0, 1, 2)]
down_units += [(u, v) for v in (-1, 1) for u in (0, 1)]
square_slots = [(u, v) for u in range(-2, 3) for v in range(-2, 3) if u * u + v * v <= 4]

left_square = [(u, 0) for u in range(-2, 3)] + [(0, 2)] + [(u, 1) for u in (-1, 0, 1)]
right_square = [(u, 0) for u in range(-2, 3)] + [(0, -2)] + [(u, -1) for u in (-1, 0, 1)]
left_cube = [(u, v) for v in (-1, 1, 0) for u in (-1, 0, 1)]
right_cube = [(u, v) for v in (1, -1, 0) for u in (-1, 0, 1)]


def given_at(u, v):
    return (v + 1) * 3 + u + 1


def unit(n, count=1):
    return pl.ds(n * UNIT, count * UNIT)


def make_kernel(rows, cols):
    def kernel(
        values, mask_x, mask_sq, out,
        staged, own, above, below, from_left, from_right,
        give_left, give_right, got_left, got_right,
        filtered, filt_above, filt_below,
        give_left2, give_right2, got_left2, got_right2,
        passing, acc, result, load_sem, out_sem, send_sem, recv_sem, pass_recv_sem, pass_send_sem,
    ):
        a, b = lax.axis_index("row"), lax.axis_index("col")

        def row(shift):
            return (lax.rem(a + shift + rows, rows), b)

        up, down = row(-1), row(1)
        left = (a, lax.rem(b + cols - 1, cols))
        right = (a, lax.rem(b + 1, cols))
        x = lax.rem(a, X)
        first, last = x == 0, x == X - 1

        loads = {}
        for c in (0, 2, 1):
            loads[c] = pltpu.make_async_copy(values.at[:, :, c], staged.at[c], load_sem.at[c])
            loads[c].start()

        barrier = pltpu.get_barrier_semaphore()

        def greet(device):
            pl.semaphore_signal(barrier, inc=1, device_id=device, device_id_type=MESH)

        for device in (up, down, left, right):
            greet(device)

        @pl.when(first)
        def _():
            greet(row(X - 1))
            greet(row(-X))

        @pl.when(last)
        def _():
            greet(row(1 - X))
            greet(row(X))

        pl.semaphore_wait(barrier, jnp.where(first | last, 6, 4))

        sent = []

        def make(src, dst, device):
            n = len(sent)
            copy = pltpu.make_async_remote_copy(
                src_ref=src, dst_ref=dst, send_sem=send_sem.at[n], recv_sem=recv_sem.at[n],
                device_id=device, device_id_type=MESH,
            )
            sent.append(copy)
            return copy

        def send(src, dst, device):
            copy = make(src, dst, device)
            copy.start()
            return [copy]

        passed = []

        def send_rows(src, src_unit, dst, dst_unit, count, goes_up, base):
            device, at_wrap, partner = (up, first, row(X - 1)) if goes_up else (down, last, row(1 - X))
            half = count * UNIT // 2
            straight = make(
                src.at[pl.ds(src_unit * UNIT, half)], dst.at[pl.ds(dst_unit * UNIT, half)], device
            )
            n = len(passed) // 2
            src_half = src.at[pl.ds(src_unit * UNIT + half, half)]
            dst_half = dst.at[pl.ds(dst_unit * UNIT + half, half)]
            hold = passing.at[pl.ds((base + dst_unit) * UNIT + half, half)]
            other = make(src_half, dst_half, device)
            k = len(sent) - 1
            detour = pltpu.make_async_remote_copy(
                src_ref=src_half, dst_ref=hold, send_sem=send_sem.at[k],
                recv_sem=pass_recv_sem.at[n], device_id=partner, device_id_type=MESH,
            )
            onward = pltpu.make_async_remote_copy(
                src_ref=hold, dst_ref=dst_half, send_sem=pass_send_sem.at[n],
                recv_sem=recv_sem.at[k], device_id=row(-X if goes_up else X), device_id_type=MESH,
            )
            passed.append((last if goes_up else first, detour, onward))
            straight.start()

            @pl.when(at_wrap)
            def _():
                detour.start()

            @pl.when(jnp.logical_not(at_wrap))
            def _():
                other.start()

            return [straight, other]

        handed = [0]

        def pass_on():
            for condition, detour, onward in passed[handed[0] : handed[0] + 2]:

                @pl.when(condition)
                def _():
                    detour.wait_recv()
                    onward.start()

            handed[0] += 2

        def blocks(ref, n):
            for l in range(2):
                for m in range(2):
                    yield l, m, ref.at[pl.ds(n * UNIT + l * BS, BS), pl.ds(m * BS, BS)]

        vertical = {}
        for c in (0, 2, 1):
            loads[c].wait()
            for ui in range(3):
                for l, m, block in blocks(own, c * 3 + ui):
                    keep = mask_x[0, 0, l, (ui * 3 + c) * 2 + m] > 0
                    value = staged[c, l, ui, m]
                    block[...] = jnp.where(keep, value, jnp.zeros_like(value))
            vertical[c] = send_rows(own, c * 3, below, c * 3, 3, True, 0)
            vertical[c] += send_rows(own, c * 3, above, c * 3, 3, False, 0)
            if c == 0:
                to_left = send(own.at[unit(c * 3, 3)], from_right, left)
            if c == 2:
                to_right = send(own.at[unit(c * 3, 3)], from_left, right)

        row_of = {-1: above, 0: own, 1: below}
        filt_of = {
            -1: (filt_above, down_units), 0: (filtered, square_units), 1: (filt_below, up_units)
        }
        factor = {
            1: lambda p: from_left[unit(p + 1)],
            -1: lambda p: from_right[unit(p + 1)],
            0: lambda p: own[unit(given_at(p, 0))],
        }

        def product_square(q, t):
            total = None
            for p in (-1, 0, 1):
                u, v = t[0] - p, t[1] - q
                if abs(u) <= 1 and abs(v) <= 1:
                    term = jnp.dot(
                        factor[q](p), row_of[p][unit(given_at(u, v))],
                        preferred_element_type=jnp.float32,
                    )
                    total = term if total is None else total + term
            return total

        def product_cube(q, t):
            total = None
            for p in (-1, 0, 1):
                u, v = t[0] - p, t[1] - q
                if u * u + v * v <= 4:
                    ref, order = filt_of[p]
                    term = jnp.dot(
                        factor[q](p), ref[unit(order.index((u, v)))],
                        preferred_element_type=jnp.float32,
                    )
                    total = term if total is None else total + term
            return total

        def give(product, q, order, targets, buffer, landing, device):
            at = order.index(targets[0])
            for n, t in enumerate(targets):
                buffer[unit(at + n)] = product(q, t).astype(jnp.bfloat16)
            span = unit(at, len(targets))
            return send(buffer.at[span], landing.at[span], device)

        def give_left_square(targets):
            return give(product_square, 1, left_square, targets, give_left, got_right, left)

        def give_right_square(targets):
            return give(product_square, -1, right_square, targets, give_right, got_left, right)

        def finish_square(t, total):
            if t in left_square:
                part = got_right[unit(left_square.index(t))].astype(jnp.float32)
                total = part if total is None else total + part
            if t in right_square:
                part = got_left[unit(right_square.index(t))].astype(jnp.float32)
                total = part if total is None else total + part
            total = total * (0.25 / BS)
            for l, m, block in blocks(filtered, square_units.index(t)):
                keep = mask_sq[0, 0, l, square_slots.index(t) * 2 + m] > 0
                value = total[l * BS : (l + 1) * BS, m * BS : (m + 1) * BS]
                block[...] = jnp.where(keep, value, jnp.zeros_like(value)).astype(jnp.bfloat16)

        def send_filtered(units_up, units_down):
            copies = []
            for units, order, landing, goes_up in (
                (units_up, up_units, filt_below, True), (units_down, down_units, filt_above, False)
            ):
                copies += send_rows(
                    filtered, square_units.index(units[0]), landing, order.index(units[0]),
                    len(units), goes_up, 9,
                )
            return copies

        def await_recv(*groups):
            for group in groups:
                for copy in group:
                    copy.wait_recv()

        await_recv(to_left, to_right)
        pass_on()
        await_recv(vertical[0])
        r_far = give_right_square([(0, -2)])
        l_mid = give_left_square([(u, 0) for u in range(-2, 3)])
        pass_on()
        await_recv(r_far)
        finish_square((0, -2), None)
        f_left = send_filtered([(0, -2)], [(0, -2)])
        await_recv(vertical[2])
        l_far = give_left_square([(0, 2)])
        r_mid = give_right_square([(u, 0) for u in range(-2, 3)])
        pass_on()
        await_recv(l_far)
        finish_square((0, 2), None)
        f_right = send_filtered([(0, 2)], [(0, 2)])
        for n, v in enumerate((-1, 1)):
            for u in (-1, 0, 1):
                acc[unit(n * 3 + u + 1)] = product_square(0, (u, v))
        await_recv(vertical[1])
        near = []
        for u in (0, -1, 1):
            near += give_left_square([(u, 1)])
            near += give_right_square([(u, -1)])
        pass_on()
        pass_on()
        await_recv(l_mid, r_mid)
        for u in range(-2, 3):
            finish_square((u, 0), product_square(0, (u, 0)))
        f_mid = send_filtered([(u, 0) for u in (-2, -1, 0)], [(u, 0) for u in (0, 1, 2)])
        await_recv(near)
        f_near = []
        for n, v in enumerate((-1, 1)):
            for u in (-1, 0, 1):
                finish_square((u, v), acc[unit(n * 3 + u + 1)])
            f_near.append(send_filtered([(u, v) for u in (-1, 0)], [(u, v) for u in (0, 1)]))

        def give_left_cube(v):
            return give(
                product_cube, 1, left_cube, [(u, v) for u in (-1, 0, 1)], give_left2, got_right2, left
            )

        def give_right_cube(v):
            return give(
                product_cube, -1, right_cube, [(u, v) for u in (-1, 0, 1)], give_right2, got_left2, right
            )

        def finish_cube(t, total):
            u, v = t
            total = total + got_right2[unit(left_cube.index(t))].astype(jnp.float32)
            total = total + got_left2[unit(right_cube.index(t))].astype(jnp.float32)
            total = 1.5 * own[unit(given_at(u, v))].astype(jnp.float32) - 0.5 * total
            for l in range(2):
                for m in range(2):
                    keep = mask_x[0, 0, l, ((u + 1) * 3 + v + 1) * 2 + m] > 0
                    value = total[l * BS : (l + 1) * BS, m * BS : (m + 1) * BS]
                    result[v + 1, l, u + 1, m] = jnp.where(keep, value, jnp.zeros_like(value)).astype(
                        jnp.bfloat16
                    )

        stores = []

        def store(v):
            copy = pltpu.make_async_copy(result.at[v + 1], out.at[:, :, v + 1], out_sem.at[v + 1])
            copy.start()
            stores.append(copy)

        await_recv(f_left)
        c_l = [give_left_cube(-1)]
        await_recv(f_right)
        c_r = [give_right_cube(1)]
        pass_on()
        await_recv(f_mid)
        c_l.append(give_left_cube(1))
        c_r.append(give_right_cube(-1))
        pass_on()
        pass_on()
        for u in (-1, 0, 1):
            acc[unit(6 + u + 1)] = product_cube(0, (u, 0))
        await_recv(f_near[0])
        c_l.append(give_left_cube(0))
        await_recv(f_near[1])
        c_r.append(give_right_cube(0))
        await_recv(c_l[0], c_l[1], c_r[0], c_r[1])
        for v in (-1, 1):
            for u in (-1, 0, 1):
                finish_cube((u, v), product_cube(0, (u, v)))
            store(v)
        await_recv(c_l[2], c_r[2])
        for u in (-1, 0, 1):
            finish_cube((u, 0), acc[unit(6 + u + 1)])
        store(0)
        for copy in sent:
            copy.wait_send()
        for condition, _, onward in passed:

            @pl.when(condition)
            def _():
                onward.wait_send()

        for copy in stores:
            copy.wait()

    return kernel


def solution(mesh):
    rows, cols = mesh.shape["row"], mesh.shape["col"]

    def units(n, dtype=jnp.bfloat16):
        return pltpu.VMEM((n * UNIT, UNIT), dtype)

    def local(values, mask_x, mask_sq):
        grid = values.reshape(2, 3, 3, 2, BS, BS)
        out = pl.pallas_call(
            make_kernel(rows, cols),
            out_shape=jax.ShapeDtypeStruct(grid.shape, jnp.bfloat16),
            in_specs=[
                pl.BlockSpec(memory_space=pl.ANY),
                pl.BlockSpec(memory_space=pltpu.SMEM),
                pl.BlockSpec(memory_space=pltpu.SMEM),
            ],
            out_specs=pl.BlockSpec(memory_space=pl.ANY),
            scratch_shapes=[
                pltpu.VMEM((3, 2, 3, 2, BS, BS), jnp.bfloat16),
                units(9), units(9), units(9), units(3), units(3),
                units(9), units(9), units(9), units(9),
                units(13), units(9), units(9),
                units(9), units(9), units(9), units(9),
                units(18),
                units(9, jnp.float32),
                pltpu.VMEM((3, 2, 3, 2, BS, BS), jnp.bfloat16),
                pltpu.SemaphoreType.DMA((3,)),
                pltpu.SemaphoreType.DMA((3,)),
                pltpu.SemaphoreType.DMA((64,)),
                pltpu.SemaphoreType.DMA((64,)),
                pltpu.SemaphoreType.DMA((16,)),
                pltpu.SemaphoreType.DMA((16,)),
            ],
            compiler_params=pltpu.CompilerParams(
                collective_id=0, has_side_effects=True, vmem_limit_bytes=60 * 2**20
            ),
        )(grid, mask_x, mask_sq)
        return out.reshape(values.shape)

    return jax.shard_map(
        local,
        mesh=mesh,
        in_specs=(
            P("row", "col", None, None, None, None),
            P("row", "col", None, None),
            P("row", "col", None, None),
        ),
        out_specs=P("row", "col", None, None, None, None),
        check_vma=False,
    )
```

time: 148 us -> 128 us (0.86)
  the two profiles are of different devices: /device:TPU:166 before, /device:TPU:31 now
where the time goes in v2:
time: 128 us
  Pallas kernels  126 us (98%)
  local copies, waits for them, and re-layouts  2.41 us (2%)
    pallas_call x1, Pallas kernels, local(): pl.pallas_call(make_kernel(rows, cols), out_shape=jax.ShapeDtypeStruct(gr...  126 us

profile of v2, /device:TPU:31, one launch (start us, length us, event | category | flops | bytes accessed | tf_op | source)
XLA Modules:
  0.0 128.2 jit_solution(4187402484538810283)
XLA Ops:
  0.0 125.8 %shard_map.37 = bf16[2,3,3,2,128,128]{5,4,3,2,1,0:T(8,128)(2,1)} custom-call(bf16[2,3,3,2,128,128]{5,4,3,2,1,0:T(8,128)(2,1)} %bitcast.3, s32[1,1,2,18]{3,2,1,0:T(2,128)} %mask_x.1, s32[1,1,2,26]{3,2,1,0:T(2,128)} %mask_sq.1), custom_call_target="tpu_custom_call" | custom-call | tf_op jit(solution)/shard_map/pallas_call | solution.py:354
  125.8 2.4 %copy.5 = bf16[1,1,2,18,128,128]{5,4,3,2,1,0:T(8,128)(2,1)} copy(bf16[1,1,2,18,128,128]{5,4,3,2,1,0:T(8,128)(2,1)} %bitcast.2) | data formatting | bytes 2359296

commit v3 on v2

--- a/solution.py
+++ b/solution.py
@@ -145,20 +145,24 @@
                 for m in range(2):
                     yield l, m, ref.at[pl.ds(n * UNIT + l * BS, BS), pl.ds(m * BS, BS)]
 
-        vertical = {}
-        for c in (0, 2, 1):
+        def mask_column(c):
             loads[c].wait()
             for ui in range(3):
                 for l, m, block in blocks(own, c * 3 + ui):
                     keep = mask_x[0, 0, l, (ui * 3 + c) * 2 + m] > 0
                     value = staged[c, l, ui, m]
                     block[...] = jnp.where(keep, value, jnp.zeros_like(value))
+
+        mask_column(0)
+        to_left = send(own.at[unit(0, 3)], from_right, left)
+        mask_column(2)
+        to_right = send(own.at[unit(6, 3)], from_left, right)
+        vertical = {}
+        for c in (0, 2, 1):
+            if c == 1:
+                mask_column(c)
             vertical[c] = send_rows(own, c * 3, below, c * 3, 3, True, 0)
             vertical[c] += send_rows(own, c * 3, above, c * 3, 3, False, 0)
-            if c == 0:
-                to_left = send(own.at[unit(c * 3, 3)], from_right, left)
-            if c == 2:
-                to_right = send(own.at[unit(c * 3, 3)], from_left, right)
 
         row_of = {-1: above, 0: own, 1: below}
         filt_of = {
@@ -237,12 +241,13 @@
                 for copy in group:
                     copy.wait_recv()
 
+        pass_on()
+        pass_on()
+        pass_on()
         await_recv(to_left, to_right)
-        pass_on()
         await_recv(vertical[0])
         r_far = give_right_square([(0, -2)])
         l_mid = give_left_square([(u, 0) for u in range(-2, 3)])
-        pass_on()
         await_recv(r_far)
         finish_square((0, -2), None)
         f_left = send_filtered([(0, -2)], [(0, -2)])
@@ -256,23 +261,25 @@
         for n, v in enumerate((-1, 1)):
             for u in (-1, 0, 1):
                 acc[unit(n * 3 + u + 1)] = product_square(0, (u, v))
+        pass_on()
         await_recv(vertical[1])
         near = []
         for u in (0, -1, 1):
             near += give_left_square([(u, 1)])
             near += give_right_square([(u, -1)])
-        pass_on()
-        pass_on()
         await_recv(l_mid, r_mid)
         for u in range(-2, 3):
             finish_square((u, 0), product_square(0, (u, 0)))
         f_mid = send_filtered([(u, 0) for u in (-2, -1, 0)], [(u, 0) for u in (0, 1, 2)])
+        pass_on()
         await_recv(near)
         f_near = []
         for n, v in enumerate((-1, 1)):
             for u in (-1, 0, 1):
                 finish_square((u, v), acc[unit(n * 3 + u + 1)])
             f_near.append(send_filtered([(u, v) for u in (-1, 0)], [(u, v) for u in (0, 1)]))
+        pass_on()
+        pass_on()
 
         def give_left_cube(v):
             return give(
@@ -308,12 +315,9 @@
         c_l = [give_left_cube(-1)]
         await_recv(f_right)
         c_r = [give_right_cube(1)]
-        pass_on()
         await_recv(f_mid)
         c_l.append(give_left_cube(1))
         c_r.append(give_right_cube(-1))
-        pass_on()
-        pass_on()
         for u in (-1, 0, 1):
             acc[unit(6 + u + 1)] = product_cube(0, (u, 0))
         await_recv(f_near[0])

time: 128 us -> 105 us (0.82)
  the two profiles are of different devices: /device:TPU:31 before, /device:TPU:32 now
where the time goes in v3:
time: 105 us; the launch traced here: 104 us
  Pallas kernels  102 us (97%)
  local copies, waits for them, and re-layouts  2.41 us (2%)
    pallas_call x1, Pallas kernels, local(): pl.pallas_call(make_kernel(rows, cols), out_shape=jax.ShapeDtypeStruct(gr...  102 us
    unnamed x1, local copies, waits for them, and re-layouts  2.41 us

profile of v3, /device:TPU:32, one launch (start us, length us, event | category | flops | bytes accessed | tf_op | source)
XLA Modules:
  0.0 104.0 jit_solution(1379653577265357801)
XLA Ops:
  0.0 101.6 %shard_map.37 = bf16[2,3,3,2,128,128]{5,4,3,2,1,0:T(8,128)(2,1)} custom-call(bf16[2,3,3,2,128,128]{5,4,3,2,1,0:T(8,128)(2,1)} %bitcast.3, s32[1,1,2,18]{3,2,1,0:T(2,128)} %mask_x.1, s32[1,1,2,26]{3,2,1,0:T(2,128)} %mask_sq.1), custom_call_target="tpu_custom_call" | custom-call | tf_op jit(solution)/shard_map/pallas_call | solution.py:358
  101.6 2.4 %copy.5 = bf16[1,1,2,18,128,128]{5,4,3,2,1,0:T(8,128)(2,1)} copy(bf16[1,1,2,18,128,128]{5,4,3,2,1,0:T(8,128)(2,1)} %bitcast.2) | data formatting | bytes 2359296

commit v4 on v3

--- a/solution.py
+++ b/solution.py
@@ -12,14 +12,12 @@
 
 square_units = [(0, -2), (0, 2)] + [(u, 0) for u in range(-2, 3)]
 square_units += [(u, -1) for u in (-1, 0, 1)] + [(u, 1) for u in (-1, 0, 1)]
-up_units = [(0, -2), (0, 2)] + [(u, 0) for u in (-2, -1, 0)]
-up_units += [(u, v) for v in (-1, 1) for u in (-1, 0)]
-down_units = [(0, -2), (0, 2)] + [(u, 0) for u in (0, 1, 2)]
-down_units += [(u, v) for v in (-1, 1) for u in (0, 1)]
+up_units = [(0, -2), (0, 2)] + [(u, v) for v in (0, -1, 1) for u in (-1, 0)] + [(-2, 0)]
+down_units = [(0, -2), (0, 2)] + [(u, v) for v in (0, -1, 1) for u in (0, 1)] + [(2, 0)]
 square_slots = [(u, v) for u in range(-2, 3) for v in range(-2, 3) if u * u + v * v <= 4]
 
-left_square = [(u, 0) for u in range(-2, 3)] + [(0, 2)] + [(u, 1) for u in (-1, 0, 1)]
-right_square = [(u, 0) for u in range(-2, 3)] + [(0, -2)] + [(u, -1) for u in (-1, 0, 1)]
+left_square = [(u, 0) for u in (-1, 0, 1)] + [(0, 2)] + [(u, 1) for u in (-1, 0, 1)]
+right_square = [(u, 0) for u in (-1, 0, 1)] + [(0, -2)] + [(u, -1) for u in (-1, 0, 1)]
 left_cube = [(u, v) for v in (-1, 1, 0) for u in (-1, 0, 1)]
 right_cube = [(u, v) for v in (1, -1, 0) for u in (-1, 0, 1)]
 
@@ -39,7 +37,7 @@
         give_left, give_right, got_left, got_right,
         filtered, filt_above, filt_below,
         give_left2, give_right2, got_left2, got_right2,
-        passing, acc, result, load_sem, out_sem, send_sem, recv_sem, pass_recv_sem, pass_send_sem,
+        passing, give_tip, tip_above, tip_below, acc, result, load_sem, out_sem, send_sem, recv_sem, pass_recv_sem, pass_send_sem,
     ):
         a, b = lax.axis_index("row"), lax.axis_index("col")
 
@@ -161,8 +159,8 @@
         for c in (0, 2, 1):
             if c == 1:
                 mask_column(c)
-            vertical[c] = send_rows(own, c * 3, below, c * 3, 3, True, 0)
-            vertical[c] += send_rows(own, c * 3, above, c * 3, 3, False, 0)
+            vertical[c] = send_rows(own, c * 3, below, c * 3, 2, True, 0)
+            vertical[c] += send_rows(own, c * 3 + 1, above, c * 3 + 1, 2, False, 0)
 
         row_of = {-1: above, 0: own, 1: below}
         filt_of = {
@@ -184,6 +182,18 @@
                         preferred_element_type=jnp.float32,
                     )
                     total = term if total is None else total + term
+            return total
+
+        def product_tip(p):
+            total = None
+            for q in (-1, 0, 1):
+                right_factor = (from_left, own, from_right)[q + 1]
+                at = given_at(p, 0) if q == 0 else p + 1
+                term = jnp.dot(
+                    (below, above)[(p + 1) // 2][unit(given_at(p, q))], right_factor[unit(at)],
+                    preferred_element_type=jnp.float32,
+                )
+                total = term if total is None else total + term
             return total
 
         def product_cube(q, t):
@@ -247,13 +257,13 @@
         await_recv(to_left, to_right)
         await_recv(vertical[0])
         r_far = give_right_square([(0, -2)])
-        l_mid = give_left_square([(u, 0) for u in range(-2, 3)])
+        l_mid = give_left_square([(u, 0) for u in (-1, 0, 1)])
         await_recv(r_far)
         finish_square((0, -2), None)
         f_left = send_filtered([(0, -2)], [(0, -2)])
         await_recv(vertical[2])
         l_far = give_left_square([(0, 2)])
-        r_mid = give_right_square([(u, 0) for u in range(-2, 3)])
+        r_mid = give_right_square([(u, 0) for u in (-1, 0, 1)])
         pass_on()
         await_recv(l_far)
         finish_square((0, 2), None)
@@ -263,14 +273,19 @@
                 acc[unit(n * 3 + u + 1)] = product_square(0, (u, v))
         pass_on()
         await_recv(vertical[1])
+        for n, p in enumerate((1, -1)):
+            give_tip[unit(n)] = product_tip(p).astype(jnp.bfloat16)
+        tips = send_rows(give_tip, 0, tip_below, 0, 1, True, 18)
+        tips += send_rows(give_tip, 1, tip_above, 0, 1, False, 18)
         near = []
         for u in (0, -1, 1):
             near += give_left_square([(u, 1)])
             near += give_right_square([(u, -1)])
+        pass_on()
         await_recv(l_mid, r_mid)
-        for u in range(-2, 3):
+        for u in (-1, 0, 1):
             finish_square((u, 0), product_square(0, (u, 0)))
-        f_mid = send_filtered([(u, 0) for u in (-2, -1, 0)], [(u, 0) for u in (0, 1, 2)])
+        f_mid = send_filtered([(u, 0) for u in (-1, 0)], [(u, 0) for u in (0, 1)])
         pass_on()
         await_recv(near)
         f_near = []
@@ -279,6 +294,12 @@
                 finish_square((u, v), acc[unit(n * 3 + u + 1)])
             f_near.append(send_filtered([(u, v) for u in (-1, 0)], [(u, v) for u in (0, 1)]))
         pass_on()
+        pass_on()
+
+        await_recv(tips)
+        for u, tip in ((-2, tip_above), (2, tip_below)):
+            finish_square((u, 0), tip[...].astype(jnp.float32))
+        f_tip = send_filtered([(-2, 0)], [(2, 0)])
         pass_on()
 
         def give_left_cube(v):
@@ -312,27 +333,30 @@
             stores.append(copy)
 
         await_recv(f_left)
-        c_l = [give_left_cube(-1)]
+        c_far = [give_left_cube(-1)]
         await_recv(f_right)
-        c_r = [give_right_cube(1)]
-        await_recv(f_mid)
-        c_l.append(give_left_cube(1))
-        c_r.append(give_right_cube(-1))
+        c_far += [give_right_cube(1)]
+        await_recv(f_mid, f_near[0])
+        c_near = [give_left_cube(0)]
+        await_recv(f_near[1])
+        c_near += [give_right_cube(0)]
+        await_recv(f_tip)
+        c_mid = [give_left_cube(1), give_right_cube(-1)]
         for u in (-1, 0, 1):
             acc[unit(6 + u + 1)] = product_cube(0, (u, 0))
-        await_recv(f_near[0])
-        c_l.append(give_left_cube(0))
-        await_recv(f_near[1])
-        c_r.append(give_right_cube(0))
-        await_recv(c_l[0], c_l[1], c_r[0], c_r[1])
-        for v in (-1, 1):
-            for u in (-1, 0, 1):
-                finish_cube((u, v), product_cube(0, (u, v)))
-            store(v)
-        await_recv(c_l[2], c_r[2])
+        await_recv(*c_far)
+        await_recv(*c_near)
         for u in (-1, 0, 1):
             finish_cube((u, 0), acc[unit(6 + u + 1)])
         store(0)
+        for v in (-1, 1):
+            for u in (-1, 0, 1):
+                acc[unit((v + 1) // 2 * 3 + u + 1)] = product_cube(0, (u, v))
+        await_recv(*c_mid)
+        for v in (-1, 1):
+            for u in (-1, 0, 1):
+                finish_cube((u, v), acc[unit((v + 1) // 2 * 3 + u + 1)])
+            store(v)
         for copy in sent:
             copy.wait_send()
         for condition, _, onward in passed:
@@ -367,10 +391,10 @@
             scratch_shapes=[
                 pltpu.VMEM((3, 2, 3, 2, BS, BS), jnp.bfloat16),
                 units(9), units(9), units(9), units(3), units(3),
-                units(9), units(9), units(9), units(9),
+                units(7), units(7), units(7), units(7),
                 units(13), units(9), units(9),
                 units(9), units(9), units(9), units(9),
-                units(18),
+                units(19), units(2), units(1), units(1),
                 units(9, jnp.float32),
                 pltpu.VMEM((3, 2, 3, 2, BS, BS), jnp.bfloat16),
                 pltpu.SemaphoreType.DMA((3,)),

time: 105 us -> 99.6 us (0.949)
  the two profiles are of different devices: /device:TPU:32 before, /device:TPU:31 now
where the time goes in v4:
time: 99.6 us; the launch traced here: 99.4 us
  Pallas kernels  97 us (97%)
  local copies, waits for them, and re-layouts  2.41 us (2%)
    pallas_call x1, Pallas kernels, local(): pl.pallas_call(make_kernel(rows, cols), out_shape=jax.ShapeDtypeStruct(gr...  97 us
    unnamed x1, local copies, waits for them, and re-layouts  2.41 us

profile of v4, /device:TPU:31, one launch (start us, length us, event | category | flops | bytes accessed | tf_op | source)
XLA Modules:
  0.0 99.4 jit_solution(4372570576741478158)
XLA Ops:
  0.0 97.0 %shard_map.37 = bf16[2,3,3,2,128,128]{5,4,3,2,1,0:T(8,128)(2,1)} custom-call(bf16[2,3,3,2,128,128]{5,4,3,2,1,0:T(8,128)(2,1)} %bitcast.3, s32[1,1,2,18]{3,2,1,0:T(2,128)} %mask_x.1, s32[1,1,2,26]{3,2,1,0:T(2,128)} %mask_sq.1), custom_call_target="tpu_custom_call" | custom-call | tf_op jit(solution)/shard_map/pallas_call | solution.py:382
  97.0 2.4 %copy.5 = bf16[1,1,2,18,128,128]{5,4,3,2,1,0:T(8,128)(2,1)} copy(bf16[1,1,2,18,128,128]{5,4,3,2,1,0:T(8,128)(2,1)} %bitcast.2) | data formatting | bytes 2359296

commit v5 on v4

--- a/solution.py
+++ b/solution.py
@@ -10,10 +10,11 @@
 MESH = pl.DeviceIdType.MESH
 X = 4
 
-square_units = [(0, -2), (0, 2)] + [(u, 0) for u in range(-2, 3)]
-square_units += [(u, -1) for u in (-1, 0, 1)] + [(u, 1) for u in (-1, 0, 1)]
-up_units = [(0, -2), (0, 2)] + [(u, v) for v in (0, -1, 1) for u in (-1, 0)] + [(-2, 0)]
-down_units = [(0, -2), (0, 2)] + [(u, v) for v in (0, -1, 1) for u in (0, 1)] + [(2, 0)]
+square_units = [(-1, 0), (0, -2), (0, 2), (0, 0), (1, 0)]
+square_units += [(u, v) for u in (-1, 0, 1) for v in (-1, 1)] + [(-2, 0), (2, 0)]
+up_units = square_units[0:4] + square_units[5:9] + [(-2, 0)]
+down_units = square_units[1:5] + square_units[7:11] + [(2, 0)]
+
 square_slots = [(u, v) for u in range(-2, 3) for v in range(-2, 3) if u * u + v * v <= 4]
 
 left_square = [(u, 0) for u in (-1, 0, 1)] + [(0, 2)] + [(u, 1) for u in (-1, 0, 1)]
@@ -32,12 +33,12 @@
 
 def make_kernel(rows, cols):
     def kernel(
-        values, mask_x, mask_sq, out,
-        staged, own, above, below, from_left, from_right,
+        values, mask_x_in, mask_sq_in, out,
+        mask_x, mask_sq, staged, own, above, below, from_left, from_right,
         give_left, give_right, got_left, got_right,
         filtered, filt_above, filt_below,
         give_left2, give_right2, got_left2, got_right2,
-        passing, give_tip, tip_above, tip_below, acc, result, load_sem, out_sem, send_sem, recv_sem, pass_recv_sem, pass_send_sem,
+        passing, give_tip, tip_above, tip_below, acc, load_sem, send_sem, recv_sem, pass_recv_sem, pass_send_sem,
     ):
         a, b = lax.axis_index("row"), lax.axis_index("col")
 
@@ -54,6 +55,12 @@
         for c in (0, 2, 1):
             loads[c] = pltpu.make_async_copy(values.at[:, :, c], staged.at[c], load_sem.at[c])
             loads[c].start()
+        masks = [
+            pltpu.make_async_copy(mask_x_in, mask_x, load_sem.at[3]),
+            pltpu.make_async_copy(mask_sq_in, mask_sq, load_sem.at[4]),
+        ]
+        for copy in masks:
+            copy.start()
 
         barrier = pltpu.get_barrier_semaphore()
 
@@ -142,6 +149,9 @@
             for l in range(2):
                 for m in range(2):
                     yield l, m, ref.at[pl.ds(n * UNIT + l * BS, BS), pl.ds(m * BS, BS)]
+
+        for copy in masks:
+            copy.wait()
 
         def mask_column(c):
             loads[c].wait()
@@ -256,22 +266,11 @@
         pass_on()
         await_recv(to_left, to_right)
         await_recv(vertical[0])
-        r_far = give_right_square([(0, -2)])
-        l_mid = give_left_square([(u, 0) for u in (-1, 0, 1)])
-        await_recv(r_far)
-        finish_square((0, -2), None)
-        f_left = send_filtered([(0, -2)], [(0, -2)])
+        far = give_right_square([(0, -2)])
+        mid = give_left_square([(u, 0) for u in (-1, 0, 1)])
         await_recv(vertical[2])
-        l_far = give_left_square([(0, 2)])
-        r_mid = give_right_square([(u, 0) for u in (-1, 0, 1)])
-        pass_on()
-        await_recv(l_far)
-        finish_square((0, 2), None)
-        f_right = send_filtered([(0, 2)], [(0, 2)])
-        for n, v in enumerate((-1, 1)):
-            for u in (-1, 0, 1):
-                acc[unit(n * 3 + u + 1)] = product_square(0, (u, v))
-        pass_on()
+        far += give_left_square([(0, 2)])
+        mid += give_right_square([(u, 0) for u in (-1, 0, 1)])
         await_recv(vertical[1])
         for n, p in enumerate((1, -1)):
             give_tip[unit(n)] = product_tip(p).astype(jnp.bfloat16)
@@ -282,24 +281,26 @@
             near += give_left_square([(u, 1)])
             near += give_right_square([(u, -1)])
         pass_on()
-        await_recv(l_mid, r_mid)
+        for n, v in enumerate((-1, 1)):
+            for u in (-1, 0, 1):
+                acc[unit(n * 3 + u + 1)] = product_square(0, (u, v))
+        await_recv(far, mid)
+        finish_square((0, -2), None)
+        finish_square((0, 2), None)
         for u in (-1, 0, 1):
             finish_square((u, 0), product_square(0, (u, 0)))
-        f_mid = send_filtered([(u, 0) for u in (-1, 0)], [(u, 0) for u in (0, 1)])
+        f_mid = send_filtered(up_units[0:4], down_units[0:4])
         pass_on()
         await_recv(near)
-        f_near = []
         for n, v in enumerate((-1, 1)):
             for u in (-1, 0, 1):
                 finish_square((u, v), acc[unit(n * 3 + u + 1)])
-            f_near.append(send_filtered([(u, v) for u in (-1, 0)], [(u, v) for u in (0, 1)]))
-        pass_on()
-        pass_on()
-
+        f_near = send_filtered(up_units[4:8], down_units[4:8])
         await_recv(tips)
         for u, tip in ((-2, tip_above), (2, tip_below)):
             finish_square((u, 0), tip[...].astype(jnp.float32))
         f_tip = send_filtered([(-2, 0)], [(2, 0)])
+        pass_on()
         pass_on()
 
         def give_left_cube(v):
@@ -321,24 +322,14 @@
                 for m in range(2):
                     keep = mask_x[0, 0, l, ((u + 1) * 3 + v + 1) * 2 + m] > 0
                     value = total[l * BS : (l + 1) * BS, m * BS : (m + 1) * BS]
-                    result[v + 1, l, u + 1, m] = jnp.where(keep, value, jnp.zeros_like(value)).astype(
+                    out[l, u + 1, v + 1, m] = jnp.where(keep, value, jnp.zeros_like(value)).astype(
                         jnp.bfloat16
                     )
 
-        stores = []
-
-        def store(v):
-            copy = pltpu.make_async_copy(result.at[v + 1], out.at[:, :, v + 1], out_sem.at[v + 1])
-            copy.start()
-            stores.append(copy)
-
-        await_recv(f_left)
-        c_far = [give_left_cube(-1)]
-        await_recv(f_right)
-        c_far += [give_right_cube(1)]
-        await_recv(f_mid, f_near[0])
+        await_recv(f_mid)
+        c_far = [give_left_cube(-1), give_right_cube(1)]
+        await_recv(f_near)
         c_near = [give_left_cube(0)]
-        await_recv(f_near[1])
         c_near += [give_right_cube(0)]
         await_recv(f_tip)
         c_mid = [give_left_cube(1), give_right_cube(-1)]
@@ -348,7 +339,6 @@
         await_recv(*c_near)
         for u in (-1, 0, 1):
             finish_cube((u, 0), acc[unit(6 + u + 1)])
-        store(0)
         for v in (-1, 1):
             for u in (-1, 0, 1):
                 acc[unit((v + 1) // 2 * 3 + u + 1)] = product_cube(0, (u, v))
@@ -356,7 +346,6 @@
         for v in (-1, 1):
             for u in (-1, 0, 1):
                 finish_cube((u, v), acc[unit((v + 1) // 2 * 3 + u + 1)])
-            store(v)
         for copy in sent:
             copy.wait_send()
         for condition, _, onward in passed:
@@ -365,8 +354,6 @@
             def _():
                 onward.wait_send()
 
-        for copy in stores:
-            copy.wait()
 
     return kernel
 
@@ -383,12 +370,13 @@
             make_kernel(rows, cols),
             out_shape=jax.ShapeDtypeStruct(grid.shape, jnp.bfloat16),
             in_specs=[
-                pl.BlockSpec(memory_space=pl.ANY),
-                pl.BlockSpec(memory_space=pltpu.SMEM),
-                pl.BlockSpec(memory_space=pltpu.SMEM),
+                pl.BlockSpec(memory_space=pltpu.HBM),
+                pl.BlockSpec(memory_space=pltpu.HBM),
+                pl.BlockSpec(memory_space=pltpu.HBM),
             ],
-            out_specs=pl.BlockSpec(memory_space=pl.ANY),
+            out_specs=pl.BlockSpec(memory_space=pltpu.VMEM),
             scratch_shapes=[
+                pltpu.SMEM(mask_x.shape, mask_x.dtype), pltpu.SMEM(mask_sq.shape, mask_sq.dtype),
                 pltpu.VMEM((3, 2, 3, 2, BS, BS), jnp.bfloat16),
                 units(9), units(9), units(9), units(3), units(3),
                 units(7), units(7), units(7), units(7),
@@ -396,16 +384,14 @@
                 units(9), units(9), units(9), units(9),
                 units(19), units(2), units(1), units(1),
                 units(9, jnp.float32),
-                pltpu.VMEM((3, 2, 3, 2, BS, BS), jnp.bfloat16),
-                pltpu.SemaphoreType.DMA((3,)),
-                pltpu.SemaphoreType.DMA((3,)),
+                pltpu.SemaphoreType.DMA((5,)),
                 pltpu.SemaphoreType.DMA((64,)),
                 pltpu.SemaphoreType.DMA((64,)),
                 pltpu.SemaphoreType.DMA((16,)),
                 pltpu.SemaphoreType.DMA((16,)),
             ],
             compiler_params=pltpu.CompilerParams(
-                collective_id=0, has_side_effects=True, vmem_limit_bytes=60 * 2**20
+                collective_id=0, has_side_effects=True, vmem_limit_bytes=52 * 2**20
             ),
         )(grid, mask_x, mask_sq)
         return out.reshape(values.shape)

time: 99.6 us -> 97.1 us (0.975)
  the two profiles are of different devices: /device:TPU:31 before, /device:TPU:32 now
where the time goes in v5:
time: 97.1 us; the launch traced here: 96.4 us
  Pallas kernels  94 us (97%)
  local copies, waits for them, and re-layouts  2.37 us (2%)
    pallas_call x1, Pallas kernels, local(): pl.pallas_call(make_kernel(rows, cols), out_shape=jax.ShapeDtypeStruct(gr...  94 us
    unnamed x5, local copies, waits for them, and re-layouts  2.37 us

profile of v5, /device:TPU:32, one launch (start us, length us, event | category | flops | bytes accessed | tf_op | source)
XLA Modules:
  0.0 96.4 jit_solution(14167338056894974325)
XLA Ops:
  0.0 0.0 copy-start
  0.0 0.7 copy-done
  0.7 0.0 copy-start.1
  0.7 0.7 copy-done.1
  1.4 94.0 %shard_map.37 = bf16[2,3,3,2,128,128]{5,4,3,2,1,0:T(8,128)(2,1)S(1)} custom-call(bf16[2,3,3,2,128,128]{5,4,3,2,1,0:T(8,128)(2,1)} %bitcast.3, s32[1,1,2,18]{3,2,1,0:T(2,128)S(1)} %copy-done, s32[1,1,2,26]{3,2,1,0:T(2,128)S(1)} %copy-done.1), custom_call_target="tpu_custom_call" | custom-call | tf_op jit(solution)/shard_map/pallas_call | solution.py:369
  95.3 1.0 %copy.5 = bf16[1,1,2,18,128,128]{5,4,3,2,1,0:T(8,128)(2,1)} copy(bf16[1,1,2,18,128,128]{5,4,3,2,1,0:T(8,128)(2,1)S(1)} %bitcast.2) | data formatting | bytes 2359296
Async XLA Ops:
  0.0 0.7 copy-start
  0.7 0.7 copy-start.1

commit v6 on v5

--- a/solution.py
+++ b/solution.py
@@ -10,17 +10,17 @@
 MESH = pl.DeviceIdType.MESH
 X = 4
 
-square_units = [(-1, 0), (0, -2), (0, 2), (0, 0), (1, 0)]
-square_units += [(u, v) for u in (-1, 0, 1) for v in (-1, 1)] + [(-2, 0), (2, 0)]
-up_units = square_units[0:4] + square_units[5:9] + [(-2, 0)]
-down_units = square_units[1:5] + square_units[7:11] + [(2, 0)]
-
+up_units = [(-1, 0), (-1, -1), (-1, 1), (-2, 0)]
+down_units = [(1, 0), (1, -1), (1, 1), (2, 0)]
+square_units = [(0, -2), (0, 0), (0, 2), (0, -1), (0, 1)] + up_units + down_units
+side_left_units = [(0, 0), (0, 2), (0, 1)]
+side_right_units = [(0, -2), (0, 0), (0, -1)]
 square_slots = [(u, v) for u in range(-2, 3) for v in range(-2, 3) if u * u + v * v <= 4]
 
 left_square = [(u, 0) for u in (-1, 0, 1)] + [(0, 2)] + [(u, 1) for u in (-1, 0, 1)]
 right_square = [(u, 0) for u in (-1, 0, 1)] + [(0, -2)] + [(u, -1) for u in (-1, 0, 1)]
-left_cube = [(u, v) for v in (-1, 1, 0) for u in (-1, 0, 1)]
-right_cube = [(u, v) for v in (1, -1, 0) for u in (-1, 0, 1)]
+left_cube = [(0, -1)] + [(u, v) for v in (0, 1) for u in (-1, 0, 1)]
+right_cube = [(0, 1)] + [(u, v) for v in (0, -1) for u in (-1, 0, 1)]
 
 
 def given_at(u, v):
@@ -38,7 +38,7 @@
         give_left, give_right, got_left, got_right,
         filtered, filt_above, filt_below,
         give_left2, give_right2, got_left2, got_right2,
-        passing, give_tip, tip_above, tip_below, acc, load_sem, send_sem, recv_sem, pass_recv_sem, pass_send_sem,
+        passing, give_tip, tip_above, tip_below, side_left, side_right, give_rim, rim_above, rim_below, acc, load_sem, send_sem, recv_sem, pass_recv_sem, pass_send_sem,
     ):
         a, b = lax.axis_index("row"), lax.axis_index("col")
 
@@ -210,13 +210,26 @@
             total = None
             for p in (-1, 0, 1):
                 u, v = t[0] - p, t[1] - q
-                if u * u + v * v <= 4:
+                if u * u + v * v <= 4 and (p == 0 or u != 0):
                     ref, order = filt_of[p]
                     term = jnp.dot(
                         factor[q](p), ref[unit(order.index((u, v)))],
                         preferred_element_type=jnp.float32,
                     )
                     total = term if total is None else total + term
+            return total
+
+        def product_rim(p, v):
+            total = None
+            for q in (-1, 0, 1):
+                ref, order = (
+                    (side_left, side_left_units), (filtered, square_units), (side_right, side_right_units)
+                )[q + 1]
+                term = jnp.dot(
+                    (below, above)[(p + 1) // 2][unit(given_at(p, q))], ref[unit(order.index((0, v - q)))],
+                    preferred_element_type=jnp.float32,
+                )
+                total = term if total is None else total + term
             return total
 
         def give(product, q, order, targets, buffer, landing, device):
@@ -274,8 +287,8 @@
         await_recv(vertical[1])
         for n, p in enumerate((1, -1)):
             give_tip[unit(n)] = product_tip(p).astype(jnp.bfloat16)
-        tips = send_rows(give_tip, 0, tip_below, 0, 1, True, 18)
-        tips += send_rows(give_tip, 1, tip_above, 0, 1, False, 18)
+        tips = send_rows(give_tip, 0, tip_below, 0, 1, True, 13)
+        tips += send_rows(give_tip, 1, tip_above, 0, 1, False, 13)
         near = []
         for u in (0, -1, 1):
             near += give_left_square([(u, 1)])
@@ -289,34 +302,45 @@
         finish_square((0, 2), None)
         for u in (-1, 0, 1):
             finish_square((u, 0), product_square(0, (u, 0)))
-        f_mid = send_filtered(up_units[0:4], down_units[0:4])
-        pass_on()
+        sides = send(filtered.at[unit(0, 2)], side_right.at[unit(0, 2)], left)
+        sides += send(filtered.at[unit(1, 2)], side_left.at[unit(0, 2)], right)
         await_recv(near)
-        for n, v in enumerate((-1, 1)):
-            for u in (-1, 0, 1):
+        for u in (0, -1, 1):
+            for n, v in enumerate((-1, 1)):
                 finish_square((u, v), acc[unit(n * 3 + u + 1)])
-        f_near = send_filtered(up_units[4:8], down_units[4:8])
+            if u == 0:
+                sides += send(filtered.at[unit(3)], side_right.at[unit(2)], left)
+                sides += send(filtered.at[unit(4)], side_left.at[unit(2)], right)
+        f_near = send_filtered(up_units[0:3], down_units[0:3])
         await_recv(tips)
         for u, tip in ((-2, tip_above), (2, tip_below)):
             finish_square((u, 0), tip[...].astype(jnp.float32))
         f_tip = send_filtered([(-2, 0)], [(2, 0)])
         pass_on()
-        pass_on()
-
-        def give_left_cube(v):
-            return give(
-                product_cube, 1, left_cube, [(u, v) for u in (-1, 0, 1)], give_left2, got_right2, left
-            )
-
-        def give_right_cube(v):
-            return give(
-                product_cube, -1, right_cube, [(u, v) for u in (-1, 0, 1)], give_right2, got_left2, right
-            )
+        await_recv(sides)
+        for n, p in enumerate((1, -1)):
+            for v in (-1, 0, 1):
+                give_rim[unit(n * 3 + v + 1)] = product_rim(p, v).astype(jnp.bfloat16)
+        rims = send_rows(give_rim, 0, rim_below, 0, 3, True, 14)
+        rims += send_rows(give_rim, 3, rim_above, 0, 3, False, 14)
+        pass_on()
+        pass_on()
+
+        def give_left_cube(targets):
+            return give(product_cube, 1, left_cube, targets, give_left2, got_right2, left)
+
+        def give_right_cube(targets):
+            return give(product_cube, -1, right_cube, targets, give_right2, got_left2, right)
 
         def finish_cube(t, total):
             u, v = t
-            total = total + got_right2[unit(left_cube.index(t))].astype(jnp.float32)
-            total = total + got_left2[unit(right_cube.index(t))].astype(jnp.float32)
+            if t in left_cube:
+                total = total + got_right2[unit(left_cube.index(t))].astype(jnp.float32)
+            if t in right_cube:
+                total = total + got_left2[unit(right_cube.index(t))].astype(jnp.float32)
+            if u != 0:
+                rim = rim_below if u == 1 else rim_above
+                total = total + rim[unit(v + 1)].astype(jnp.float32)
             total = 1.5 * own[unit(given_at(u, v))].astype(jnp.float32) - 0.5 * total
             for l in range(2):
                 for m in range(2):
@@ -326,26 +350,20 @@
                         jnp.bfloat16
                     )
 
-        await_recv(f_mid)
-        c_far = [give_left_cube(-1), give_right_cube(1)]
+        c_parts = give_left_cube([(0, -1)]) + give_right_cube([(0, 1)])
         await_recv(f_near)
-        c_near = [give_left_cube(0)]
-        c_near += [give_right_cube(0)]
+        line = [(u, 0) for u in (-1, 0, 1)]
+        c_parts += give_left_cube(line) + give_right_cube(line)
         await_recv(f_tip)
-        c_mid = [give_left_cube(1), give_right_cube(-1)]
-        for u in (-1, 0, 1):
-            acc[unit(6 + u + 1)] = product_cube(0, (u, 0))
-        await_recv(*c_far)
-        await_recv(*c_near)
-        for u in (-1, 0, 1):
-            finish_cube((u, 0), acc[unit(6 + u + 1)])
-        for v in (-1, 1):
+        c_parts += give_left_cube([(u, 1) for u in (-1, 0, 1)])
+        c_parts += give_right_cube([(u, -1) for u in (-1, 0, 1)])
+        for v in (-1, 0, 1):
             for u in (-1, 0, 1):
-                acc[unit((v + 1) // 2 * 3 + u + 1)] = product_cube(0, (u, v))
-        await_recv(*c_mid)
-        for v in (-1, 1):
+                acc[unit((v + 1) * 3 + u + 1)] = product_cube(0, (u, v))
+        await_recv(rims, c_parts)
+        for v in (-1, 0, 1):
             for u in (-1, 0, 1):
-                finish_cube((u, v), acc[unit((v + 1) // 2 * 3 + u + 1)])
+                finish_cube((u, v), acc[unit((v + 1) * 3 + u + 1)])
         for copy in sent:
             copy.wait_send()
         for condition, _, onward in passed:
@@ -380,9 +398,10 @@
                 pltpu.VMEM((3, 2, 3, 2, BS, BS), jnp.bfloat16),
                 units(9), units(9), units(9), units(3), units(3),
                 units(7), units(7), units(7), units(7),
-                units(13), units(9), units(9),
-                units(9), units(9), units(9), units(9),
-                units(19), units(2), units(1), units(1),
+                units(13), units(4), units(4),
+                units(7), units(7), units(7), units(7),
+                units(17), units(2), units(1), units(1),
+                units(3), units(3), units(6), units(3), units(3),
                 units(9, jnp.float32),
                 pltpu.SemaphoreType.DMA((5,)),
                 pltpu.SemaphoreType.DMA((64,)),

time: 97.1 us -> 93.3 us (0.961)
  Pallas kernels: 94 us -> 89.9 us
    pallas_call x1, Pallas kernels: 94 us -> 89.9 us  [local(): pl.pallas_call(make_kernel(rows, cols), out_shape=jax.ShapeDtypeStruct(gr...]
where the time goes in v6:
time: 93.3 us; the launch traced here: 92.2 us
  Pallas kernels  89.9 us (96%)
  local copies, waits for them, and re-layouts  2.37 us (3%)
    pallas_call x1, Pallas kernels, local(): pl.pallas_call(make_kernel(rows, cols), out_shape=jax.ShapeDtypeStruct(gr...  89.9 us
    unnamed x5, local copies, waits for them, and re-layouts  2.37 us

profile of v6, /device:TPU:32, one launch (start us, length us, event | category | flops | bytes accessed | tf_op | source)
XLA Modules:
  0.0 92.2 jit_solution(3496525815088502979)
XLA Ops:
  0.0 0.0 copy-start
  0.0 0.7 copy-done
  0.7 0.0 copy-start.1
  0.7 0.7 copy-done.1
  1.4 89.9 %shard_map.37 = bf16[2,3,3,2,128,128]{5,4,3,2,1,0:T(8,128)(2,1)S(1)} custom-call(bf16[2,3,3,2,128,128]{5,4,3,2,1,0:T(8,128)(2,1)} %bitcast.3, s32[1,1,2,18]{3,2,1,0:T(2,128)S(1)} %copy-done, s32[1,1,2,26]{3,2,1,0:T(2,128)S(1)} %copy-done.1), custom_call_target="tpu_custom_call" | custom-call | tf_op jit(solution)/shard_map/pallas_call | solution.py:387
  91.2 1.0 %copy.5 = bf16[1,1,2,18,128,128]{5,4,3,2,1,0:T(8,128)(2,1)} copy(bf16[1,1,2,18,128,128]{5,4,3,2,1,0:T(8,128)(2,1)S(1)} %bitcast.2) | data formatting | bytes 2359296
Async XLA Ops:
  0.0 0.7 copy-start
  0.7 0.7 copy-start.1

commit v7 on v6

--- a/solution.py
+++ b/solution.py
@@ -9,6 +9,8 @@
 UNIT = 2 * BS
 MESH = pl.DeviceIdType.MESH
 X = 4
+RUN = 8
+AROUND = 8
 
 up_units = [(-1, 0), (-1, -1), (-1, 1), (-2, 0)]
 down_units = [(1, 0), (1, -1), (1, 1), (2, 0)]
@@ -38,7 +40,8 @@
         give_left, give_right, got_left, got_right,
         filtered, filt_above, filt_below,
         give_left2, give_right2, got_left2, got_right2,
-        passing, give_tip, tip_above, tip_below, side_left, side_right, give_rim, rim_above, rim_below, acc, load_sem, send_sem, recv_sem, pass_recv_sem, pass_send_sem,
+        passing, give_tip, tip_above, tip_below, side_left, side_right, give_rim, rim_above, rim_below,
+        passing_side, acc, load_sem, send_sem, recv_sem, pass_recv_sem, pass_send_sem, around_recv_sem, around_send_sem,
     ):
         a, b = lax.axis_index("row"), lax.axis_index("col")
 
@@ -50,6 +53,10 @@
         right = (a, lax.rem(b + 1, cols))
         x = lax.rem(a, X)
         first, last = x == 0, x == X - 1
+        at_end = first | last
+        run = lax.rem(b, RUN)
+        wraps_left, wraps_right = run == 0, run == RUN - 1
+        inward = jnp.where(x < X // 2, 1, -1)
 
         loads = {}
         for c in (0, 2, 1):
@@ -80,16 +87,27 @@
             greet(row(1 - X))
             greet(row(X))
 
-        pl.semaphore_wait(barrier, jnp.where(first | last, 6, 4))
+        @pl.when(at_end & wraps_left)
+        def _():
+            greet((row(inward)[0], left[1]))
+
+        @pl.when(at_end & wraps_right)
+        def _():
+            greet((row(inward)[0], right[1]))
+
+        pl.semaphore_wait(barrier, jnp.where(at_end, 6, jnp.where(wraps_left | wraps_right, 5, 4)))
 
         sent = []
+
+        def remote(src, dst, gone, come, device):
+            return pltpu.make_async_remote_copy(
+                src_ref=src, dst_ref=dst, send_sem=gone, recv_sem=come, device_id=device,
+                device_id_type=MESH,
+            )
 
         def make(src, dst, device):
             n = len(sent)
-            copy = pltpu.make_async_remote_copy(
-                src_ref=src, dst_ref=dst, send_sem=send_sem.at[n], recv_sem=recv_sem.at[n],
-                device_id=device, device_id_type=MESH,
-            )
+            copy = remote(src, dst, send_sem.at[n], recv_sem.at[n], device)
             sent.append(copy)
             return copy
 
@@ -145,6 +163,49 @@
 
             handed[0] += 2
 
+        side_relays = {True: [], False: []}
+
+        def send_side(src, dst, at, count, goes_left, hold_at):
+            size = count * UNIT
+            lead = size - size * AROUND // 16
+            device, at_wrap = (left, wraps_left) if goes_left else (right, wraps_right)
+
+            def part(start, length):
+                span = pl.ds(at * UNIT + start, length)
+                return src.at[span], dst.at[span]
+
+            plain = make(*part(0, size), device)
+            n = len(sent) - 1
+            gone, come = send_sem.at[n], recv_sem.at[n]
+            straight = remote(*part(0, lead), gone, come, device)
+            src_ref, dst_ref = part(lead, size - lead)
+            hold = passing_side.at[pl.ds(hold_at * UNIT, size - lead)]
+            k = len(side_relays[goes_left])
+            there = remote(src_ref, hold, gone, around_recv_sem.at[k], row(inward))
+            back = (lax.rem(a + rows - inward, rows), device[1])
+            on = remote(hold, dst_ref, around_send_sem.at[k], come, back)
+            side_relays[goes_left].append((there, on))
+
+            @pl.when(at_wrap & at_end)
+            def _():
+                there.start()
+                straight.start()
+
+            @pl.when(jnp.logical_not(at_wrap & at_end))
+            def _():
+                plain.start()
+
+            return [plain]
+
+        def pass_around(start, stop):
+            for goes_left, at_wrap in ((True, wraps_left), (False, wraps_right)):
+
+                @pl.when(at_wrap & jnp.logical_not(at_end))
+                def _():
+                    for there, on in side_relays[goes_left][start:stop]:
+                        there.wait_recv()
+                        on.start()
+
         def blocks(ref, n):
             for l in range(2):
                 for m in range(2):
@@ -232,18 +293,20 @@
                 total = term if total is None else total + term
             return total
 
-        def give(product, q, order, targets, buffer, landing, device):
+        def give(product, q, order, targets, buffer, landing, device, hold_at=None):
             at = order.index(targets[0])
             for n, t in enumerate(targets):
                 buffer[unit(at + n)] = product(q, t).astype(jnp.bfloat16)
+            if hold_at is not None:
+                return send_side(buffer, landing, at, len(targets), q == 1, hold_at)
             span = unit(at, len(targets))
             return send(buffer.at[span], landing.at[span], device)
 
-        def give_left_square(targets):
-            return give(product_square, 1, left_square, targets, give_left, got_right, left)
-
-        def give_right_square(targets):
-            return give(product_square, -1, right_square, targets, give_right, got_left, right)
+        def give_left_square(targets, hold_at=None):
+            return give(product_square, 1, left_square, targets, give_left, got_right, left, hold_at)
+
+        def give_right_square(targets, hold_at=None):
+            return give(product_square, -1, right_square, targets, give_right, got_left, right, hold_at)
 
         def finish_square(t, total):
             if t in left_square:
@@ -274,16 +337,22 @@
                 for copy in group:
                     copy.wait_recv()
 
+        def give_left_cube(targets, hold_at=None):
+            return give(product_cube, 1, left_cube, targets, give_left2, got_right2, left, hold_at)
+
+        def give_right_cube(targets, hold_at=None):
+            return give(product_cube, -1, right_cube, targets, give_right2, got_left2, right, hold_at)
+
         pass_on()
         pass_on()
         pass_on()
         await_recv(to_left, to_right)
         await_recv(vertical[0])
         far = give_right_square([(0, -2)])
-        mid = give_left_square([(u, 0) for u in (-1, 0, 1)])
+        mid = give_left_square([(u, 0) for u in (-1, 0, 1)], 0)
         await_recv(vertical[2])
         far += give_left_square([(0, 2)])
-        mid += give_right_square([(u, 0) for u in (-1, 0, 1)])
+        mid += give_right_square([(u, 0) for u in (-1, 0, 1)], 0)
         await_recv(vertical[1])
         for n, p in enumerate((1, -1)):
             give_tip[unit(n)] = product_tip(p).astype(jnp.bfloat16)
@@ -291,12 +360,12 @@
         tips += send_rows(give_tip, 1, tip_above, 0, 1, False, 13)
         near = []
         for u in (0, -1, 1):
-            near += give_left_square([(u, 1)])
-            near += give_right_square([(u, -1)])
-        pass_on()
+            near += give_left_square([(u, 1)], 4 + u)
+            near += give_right_square([(u, -1)], 4 + u)
         for n, v in enumerate((-1, 1)):
             for u in (-1, 0, 1):
                 acc[unit(n * 3 + u + 1)] = product_square(0, (u, v))
+        pass_around(0, 1)
         await_recv(far, mid)
         finish_square((0, -2), None)
         finish_square((0, 2), None)
@@ -304,6 +373,8 @@
             finish_square((u, 0), product_square(0, (u, 0)))
         sides = send(filtered.at[unit(0, 2)], side_right.at[unit(0, 2)], left)
         sides += send(filtered.at[unit(1, 2)], side_left.at[unit(0, 2)], right)
+        pass_on()
+        pass_around(1, 4)
         await_recv(near)
         for u in (0, -1, 1):
             for n, v in enumerate((-1, 1)):
@@ -316,6 +387,8 @@
         for u, tip in ((-2, tip_above), (2, tip_below)):
             finish_square((u, 0), tip[...].astype(jnp.float32))
         f_tip = send_filtered([(-2, 0)], [(2, 0)])
+        c_parts = give_left_cube([(0, -1)]) + give_right_cube([(0, 1)])
+        pass_on()
         pass_on()
         await_recv(sides)
         for n, p in enumerate((1, -1)):
@@ -323,14 +396,6 @@
                 give_rim[unit(n * 3 + v + 1)] = product_rim(p, v).astype(jnp.bfloat16)
         rims = send_rows(give_rim, 0, rim_below, 0, 3, True, 14)
         rims += send_rows(give_rim, 3, rim_above, 0, 3, False, 14)
-        pass_on()
-        pass_on()
-
-        def give_left_cube(targets):
-            return give(product_cube, 1, left_cube, targets, give_left2, got_right2, left)
-
-        def give_right_cube(targets):
-            return give(product_cube, -1, right_cube, targets, give_right2, got_left2, right)
 
         def finish_cube(t, total):
             u, v = t
@@ -350,13 +415,14 @@
                         jnp.bfloat16
                     )
 
-        c_parts = give_left_cube([(0, -1)]) + give_right_cube([(0, 1)])
         await_recv(f_near)
         line = [(u, 0) for u in (-1, 0, 1)]
-        c_parts += give_left_cube(line) + give_right_cube(line)
+        c_parts += give_left_cube(line, 6) + give_right_cube(line, 6)
+        pass_on()
         await_recv(f_tip)
-        c_parts += give_left_cube([(u, 1) for u in (-1, 0, 1)])
-        c_parts += give_right_cube([(u, -1) for u in (-1, 0, 1)])
+        c_parts += give_left_cube([(u, 1) for u in (-1, 0, 1)], 9)
+        c_parts += give_right_cube([(u, -1) for u in (-1, 0, 1)], 9)
+        pass_around(4, 6)
         for v in (-1, 0, 1):
             for u in (-1, 0, 1):
                 acc[unit((v + 1) * 3 + u + 1)] = product_cube(0, (u, v))
@@ -366,6 +432,13 @@
                 finish_cube((u, v), acc[unit((v + 1) * 3 + u + 1)])
         for copy in sent:
             copy.wait_send()
+        for goes_left, at_wrap in ((True, wraps_left), (False, wraps_right)):
+
+            @pl.when(at_wrap & jnp.logical_not(at_end))
+            def _():
+                for _, on in side_relays[goes_left]:
+                    on.wait_send()
+
         for condition, _, onward in passed:
 
             @pl.when(condition)
@@ -402,12 +475,14 @@
                 units(7), units(7), units(7), units(7),
                 units(17), units(2), units(1), units(1),
                 units(3), units(3), units(6), units(3), units(3),
-                units(9, jnp.float32),
+                units(12), units(9, jnp.float32),
                 pltpu.SemaphoreType.DMA((5,)),
                 pltpu.SemaphoreType.DMA((64,)),
                 pltpu.SemaphoreType.DMA((64,)),
                 pltpu.SemaphoreType.DMA((16,)),
                 pltpu.SemaphoreType.DMA((16,)),
+                pltpu.SemaphoreType.DMA((6,)),
+                pltpu.SemaphoreType.DMA((6,)),
             ],
             compiler_params=pltpu.CompilerParams(
                 collective_id=0, has_side_effects=True, vmem_limit_bytes=52 * 2**20

time: 93.3 us -> 86 us (0.922)
  Pallas kernels: 89.9 us -> 83.5 us
    pallas_call x1, Pallas kernels: 89.9 us -> 83.5 us  [local(): pl.pallas_call(make_kernel(rows, cols), out_shape=jax.ShapeDtypeStruct(gr...]
where the time goes in v7:
time: 86 us; the launch traced here: 85.9 us
  Pallas kernels  83.5 us (97%)
  local copies, waits for them, and re-layouts  2.37 us (3%)
    pallas_call x1, Pallas kernels, local(): pl.pallas_call(make_kernel(rows, cols), out_shape=jax.ShapeDtypeStruct(gr...  83.5 us
    unnamed x5, local copies, waits for them, and re-layouts  2.37 us

profile of v7, /device:TPU:32, one launch (start us, length us, event | category | flops | bytes accessed | tf_op | source)
XLA Modules:
  0.0 85.9 jit_solution(15810774354255765659)
XLA Ops:
  0.0 0.0 copy-start
  0.0 0.7 copy-done
  0.7 0.0 copy-start.1
  0.7 0.7 copy-done.1
  1.4 83.5 %shard_map.37 = bf16[2,3,3,2,128,128]{5,4,3,2,1,0:T(8,128)(2,1)S(1)} custom-call(bf16[2,3,3,2,128,128]{5,4,3,2,1,0:T(8,128)(2,1)} %bitcast.3, s32[1,1,2,18]{3,2,1,0:T(2,128)S(1)} %copy-done, s32[1,1,2,26]{3,2,1,0:T(2,128)S(1)} %copy-done.1), custom_call_target="tpu_custom_call" | custom-call | tf_op jit(solution)/shard_map/pallas_call | solution.py:460
  84.8 1.0 %copy.5 = bf16[1,1,2,18,128,128]{5,4,3,2,1,0:T(8,128)(2,1)} copy(bf16[1,1,2,18,128,128]{5,4,3,2,1,0:T(8,128)(2,1)S(1)} %bitcast.2) | data formatting | bytes 2359296
Async XLA Ops:
  0.0 0.7 copy-start
  0.7 0.7 copy-start.1

commit v8 on v7

--- a/solution.py
+++ b/solution.py
@@ -416,13 +416,13 @@
                     )
 
         await_recv(f_near)
-        line = [(u, 0) for u in (-1, 0, 1)]
-        c_parts += give_left_cube(line, 6) + give_right_cube(line, 6)
+        for u in (-1, 0, 1):
+            c_parts += give_left_cube([(u, 0)], 7 + u) + give_right_cube([(u, 0)], 7 + u)
         pass_on()
         await_recv(f_tip)
-        c_parts += give_left_cube([(u, 1) for u in (-1, 0, 1)], 9)
-        c_parts += give_right_cube([(u, -1) for u in (-1, 0, 1)], 9)
-        pass_around(4, 6)
+        for u in (-1, 0, 1):
+            c_parts += give_left_cube([(u, 1)], 10 + u) + give_right_cube([(u, -1)], 10 + u)
+        pass_around(4, 10)
         for v in (-1, 0, 1):
             for u in (-1, 0, 1):
                 acc[unit((v + 1) * 3 + u + 1)] = product_cube(0, (u, v))
@@ -481,8 +481,8 @@
                 pltpu.SemaphoreType.DMA((64,)),
                 pltpu.SemaphoreType.DMA((16,)),
                 pltpu.SemaphoreType.DMA((16,)),
-                pltpu.SemaphoreType.DMA((6,)),
-                pltpu.SemaphoreType.DMA((6,)),
+                pltpu.SemaphoreType.DMA((10,)),
+                pltpu.SemaphoreType.DMA((10,)),
             ],
             compiler_params=pltpu.CompilerParams(
                 collective_id=0, has_side_effects=True, vmem_limit_bytes=52 * 2**20

time: 86 us -> 85 us (0.988)
  Pallas kernels: 83.5 us -> 82.5 us
    pallas_call x1, Pallas kernels: 83.5 us -> 82.5 us  [local(): pl.pallas_call(make_kernel(rows, cols), out_shape=jax.ShapeDtypeStruct(gr...]
where the time goes in v8:
time: 85 us; the launch traced here: 84.9 us
  Pallas kernels  82.5 us (97%)
  local copies, waits for them, and re-layouts  2.37 us (3%)
    pallas_call x1, Pallas kernels, local(): pl.pallas_call(make_kernel(rows, cols), out_shape=jax.ShapeDtypeStruct(gr...  82.5 us
    unnamed x5, local copies, waits for them, and re-layouts  2.37 us

profile of v8, /device:TPU:32, one launch (start us, length us, event | category | flops | bytes accessed | tf_op | source)
XLA Modules:
  0.0 84.9 jit_solution(7193637927048663185)
XLA Ops:
  0.0 0.0 copy-start
  0.0 0.7 copy-done
  0.7 0.0 copy-start.1
  0.7 0.7 copy-done.1
  1.4 82.5 %shard_map.37 = bf16[2,3,3,2,128,128]{5,4,3,2,1,0:T(8,128)(2,1)S(1)} custom-call(bf16[2,3,3,2,128,128]{5,4,3,2,1,0:T(8,128)(2,1)} %bitcast.3, s32[1,1,2,18]{3,2,1,0:T(2,128)S(1)} %copy-done, s32[1,1,2,26]{3,2,1,0:T(2,128)S(1)} %copy-done.1), custom_call_target="tpu_custom_call" | custom-call | tf_op jit(solution)/shard_map/pallas_call | solution.py:460
  83.9 1.0 %copy.5 = bf16[1,1,2,18,128,128]{5,4,3,2,1,0:T(8,128)(2,1)} copy(bf16[1,1,2,18,128,128]{5,4,3,2,1,0:T(8,128)(2,1)S(1)} %bitcast.2) | data formatting | bytes 2359296
Async XLA Ops:
  0.0 0.7 copy-start
  0.7 0.7 copy-start.1

commit v9 on v8

--- a/solution.py
+++ b/solution.py
@@ -416,9 +416,9 @@
                     )
 
         await_recv(f_near)
+        pass_on()
         for u in (-1, 0, 1):
             c_parts += give_left_cube([(u, 0)], 7 + u) + give_right_cube([(u, 0)], 7 + u)
-        pass_on()
         await_recv(f_tip)
         for u in (-1, 0, 1):
             c_parts += give_left_cube([(u, 1)], 10 + u) + give_right_cube([(u, -1)], 10 + u)

time: 85 us -> 89.1 us (1.048)
  Pallas kernels: 82.5 us -> 86.6 us
    pallas_call x1, Pallas kernels: 82.5 us -> 86.6 us  [local(): pl.pallas_call(make_kernel(rows, cols), out_shape=jax.ShapeDtypeStruct(gr...]
where the time goes in v9:
time: 89.1 us; the launch traced here: 89 us
  Pallas kernels  86.6 us (97%)
  local copies, waits for them, and re-layouts  2.37 us (3%)
    pallas_call x1, Pallas kernels, local(): pl.pallas_call(make_kernel(rows, cols), out_shape=jax.ShapeDtypeStruct(gr...  86.6 us
    unnamed x5, local copies, waits for them, and re-layouts  2.37 us

profile of v9, /device:TPU:32, one launch (start us, length us, event | category | flops | bytes accessed | tf_op | source)
XLA Modules:
  0.0 89.0 jit_solution(15449476958876040820)
XLA Ops:
  0.0 0.0 copy-start
  0.0 0.7 copy-done
  0.7 0.0 copy-start.1
  0.7 0.7 copy-done.1
  1.4 86.6 %shard_map.37 = bf16[2,3,3,2,128,128]{5,4,3,2,1,0:T(8,128)(2,1)S(1)} custom-call(bf16[2,3,3,2,128,128]{5,4,3,2,1,0:T(8,128)(2,1)} %bitcast.3, s32[1,1,2,18]{3,2,1,0:T(2,128)S(1)} %copy-done, s32[1,1,2,26]{3,2,1,0:T(2,128)S(1)} %copy-done.1), custom_call_target="tpu_custom_call" | custom-call | tf_op jit(solution)/shard_map/pallas_call | solution.py:460
  88.0 1.0 %copy.5 = bf16[1,1,2,18,128,128]{5,4,3,2,1,0:T(8,128)(2,1)} copy(bf16[1,1,2,18,128,128]{5,4,3,2,1,0:T(8,128)(2,1)S(1)} %bitcast.2) | data formatting | bytes 2359296
Async XLA Ops:
  0.0 0.7 copy-start
  0.7 0.7 copy-start.1
